TPU v7x, 128 devices: a whole 4x4x4 slice. The times are simulated.
128 devices in a mesh: gx: 8 (over x, y_hi), gy: 16 (over z, y_lo, core).
Axes of the slice: x: 4, y: 4 (y_hi: 2, y_lo: 2; y = y_hi * 2 + y_lo), z: 4, core: 2. Of those that a mesh axis runs over, the one named last changes fastest.
Arguments:
- basis: float32 [1, 32, 64, 128, 128], P(None, 'gx', 'gy'), may hold values from 0 to 1, as said below
- trans: float32 [3, 1, 2048, 4096], P(None, None, 'gx', 'gy'), may hold values from 0.05 to 0.5
- reaction: float32 [1, 2048, 4096], P(None, 'gx', 'gy'), may hold values from 0.01 to 0.2
- support: int32 [32, 64, 128, 128], P('gx', 'gy'), may hold values from 0 to 1, as said below
- codes: int32 [32, 64, 128, 128], P('gx', 'gy'), may hold values from 0 to 8, as said below
- active: int32 [1, 32, 64, 128, 128], P(None, 'gx', 'gy'), may hold values from 0 to 1, as said below
- owner: int32 [2048, 1], P(('gx', 'gy')), may hold values from 0 to 7; in each aligned block of 16 rows (0 to 15, 16 to 31, ...) at most 4 rows name the same one
Outputs:
- smoothed: float32 [1, 32, 64, 128, 128], P(None, 'gx', 'gy')
- coarse_rows: float32 [4096, 9], P(('gx', 'gy'))
Inputs may be any that keep to these rules, and one draw needn't show every extreme that they name: `support`: 1 on every cell inside the grid that codes marks 4; 0 on each window's outermost cycle of cells and outside the grid. `codes`: inside the grid, (dx + 1) * 3 + (dy + 1), where (dx, dy) is the offset of the coarse block holding the cell from the window's own block, the same block for a cell in every window; 4 outside the grid. `active`: the same for a cell in every window that holds it; 0 outside the grid. `basis`: nonnegative; 0 wherever support or active is 0; positive on the active cells that codes marks 4. The coarse blocks of one device name each owner at most 4 times.
All inputs are finite; a program needn't handle non-finite values.
Results may differ from a plain program's by a relative error of at most 0.0003.
Values sent between devices are 32-bit elements; how exact they have to be, the bound alone decides.
A program may use at most 128 MiB of HBM per device.

v0:
```python
import jax
import jax.numpy as jnp
from jax import lax
from jax.sharding import PartitionSpec as P

ITERS = 3


relaxation = 2.0 / 3.0


def with_halo(cells, sides, width):
    for axis, dim in sides:
        count = lax.axis_size(axis)
        ends = count - 1
        head = lax.slice_in_dim(cells, 0, width, axis=dim)
        tail = lax.slice_in_dim(cells, cells.shape[dim] - width, cells.shape[dim], axis=dim)
        cells = jnp.concatenate(
            [
                lax.ppermute(tail, axis, [(i, (i + 1) % count) for i in range(ends)]),
                cells,
                lax.ppermute(head, axis, [((i + 1) % count, i) for i in range(ends)]),
            ],
            axis=dim,
        )
    return cells


def cut_windows(whole, count_x, count_y, block_width):
    leading = whole.shape[:-2]
    pieces = whole.reshape(leading + (count_x + 1, block_width, count_y + 1, block_width))
    row_pairs = jnp.concatenate([pieces[..., :-1, :, :, :], pieces[..., 1:, :, :, :]], axis=-3)
    paired = jnp.concatenate([row_pairs[..., :-1, :], row_pairs[..., 1:, :]], axis=-1)
    return jnp.swapaxes(paired, -3, -2)


def spread_windows(blocks, count_x, count_y, block_width):
    leading = blocks.shape[:-4]
    summed = None
    for half_x in range(2):
        for half_y in range(2):
            quarter = blocks[
                ...,
                half_x * block_width : (half_x + 1) * block_width,
                half_y * block_width : (half_y + 1) * block_width,
            ]
            widths = [(0, 0)] * len(leading) + [
                (half_x, 1 - half_x),
                (half_y, 1 - half_y),
                (0, 0),
                (0, 0),
            ]
            placed = jnp.pad(quarter, widths)
            summed = placed if summed is None else summed + placed
    summed = jnp.swapaxes(summed, -3, -2)
    return summed.reshape(leading + ((count_x + 1) * block_width, (count_y + 1) * block_width))


def next_cell(cell_values, along):
    extent = cell_values.shape[along]
    upper_part = lax.slice_in_dim(cell_values, 1, extent, axis=along)
    return jnp.concatenate(
        [upper_part, jnp.zeros_like(lax.slice_in_dim(cell_values, 0, 1, axis=along))], axis=along
    )


def prior_cell(cell_values, along):
    extent = cell_values.shape[along]
    lower_part = lax.slice_in_dim(cell_values, 0, extent - 1, axis=along)
    return jnp.concatenate(
        [jnp.zeros_like(lax.slice_in_dim(cell_values, 0, 1, axis=along)), lower_part], axis=along
    )


def operate(cell_values, trans_win, reaction_win):
    dims_count = cell_values.ndim
    result = reaction_win * cell_values
    for face_index, along in ((0, dims_count - 2), (1, dims_count - 1), (2, 0)):
        face_flux = trans_win[face_index] * (cell_values - next_cell(cell_values, along))
        result = result + face_flux - prior_cell(face_flux, along)
    return result


def diagonal_scale(trans_win, reaction_win):
    dims_count = reaction_win.ndim
    summed = reaction_win
    for face_index, along in ((0, dims_count - 2), (1, dims_count - 1), (2, 0)):
        summed = summed + trans_win[face_index] + prior_cell(trans_win[face_index], along)
    return summed


def fold_band(haloed, along, cells, block_width, reach):
    extent = cells + block_width
    center = lax.slice_in_dim(haloed, reach, reach + extent, axis=along)
    upper_band = lax.slice_in_dim(haloed, reach + extent, 2 * reach + extent, axis=along)
    lower_band = lax.slice_in_dim(haloed, 0, reach, axis=along)
    upper_pads = [(0, 0)] * haloed.ndim
    upper_pads[along] = (cells, extent - cells - reach)
    lower_pads = [(0, 0)] * haloed.ndim
    lower_pads[along] = (block_width - reach, extent - block_width)
    return center + jnp.pad(upper_band, upper_pads) + jnp.pad(lower_band, lower_pads)


def fold_bands(haloed, cells_x, cells_y, block_width, reach):
    return fold_band(
        fold_band(haloed, 1, cells_x, block_width, reach), 2, cells_y, block_width, reach
    )


def assemble_rows(column_halo, count_x, count_y):
    picked = []
    for code in range(9):
        shift_x = code // 3 - 1
        shift_y = code % 3 - 1
        picked.append(
            column_halo[
                8 - code, 1 + shift_x : 1 + shift_x + count_x, 1 + shift_y : 1 + shift_y + count_y
            ]
        )
    return jnp.stack(picked, axis=-1)


def ranks(owners):
    count_rows = owners.shape[0]
    same_owner = owners[:, None] == owners[None, :]
    earlier = jnp.arange(count_rows)[None, :] < jnp.arange(count_rows)[:, None]
    return jnp.sum(jnp.where(same_owner & earlier, 1, 0), axis=1).astype(jnp.int32)


def local(basis, trans, reaction, support, codes, active, owner):
    block_width = basis.shape[-1] // 2
    margin = block_width // 2
    layers = basis.shape[0]
    count_x = basis.shape[1]
    count_y = basis.shape[2]
    cells_x = count_x * block_width
    cells_y = count_y * block_width
    trans_ext, reaction_ext = (
        with_halo(trans, (("gx", 2), ("gy", 3)), margin),
        with_halo(reaction[None], (("gx", 2), ("gy", 3)), margin),
    )
    trans_win = cut_windows(trans_ext, count_x, count_y, block_width)
    reaction_win = cut_windows(reaction_ext, count_x, count_y, block_width)[0]
    live = active.astype(jnp.float32)
    kept = support.astype(jnp.float32)[None] * live
    scale = diagonal_scale(trans_win, reaction_win) + 1.0 - live
    current = basis
    for sweep in range(ITERS):
        applied = operate(current, trans_win, reaction_win)
        raw = kept * (current - relaxation * applied / scale)
        partial_value = spread_windows(raw, count_x, count_y, block_width)
        haloed = with_halo(partial_value, (("gx", 1), ("gy", 2)), margin)
        folded = fold_bands(haloed, cells_x, cells_y, block_width, margin)
        owned = folded[:, margin : margin + cells_x, margin : margin + cells_y]
        totals = with_halo(owned, (("gx", 1), ("gy", 2)), margin)
        total_win = cut_windows(totals, count_x, count_y, block_width)
        current = raw / (total_win + 1.0 - live)
    applied = operate(current, trans_win, reaction_win)
    weighted = jnp.sum(applied * live, axis=0)
    sums = [jnp.sum(jnp.where(codes == code, weighted, 0.0), axis=(2, 3)) for code in range(9)]
    columns = jnp.stack(sums, axis=0) / (block_width * layers)
    column_halo = with_halo(columns, (("gx", 1), ("gy", 2)), 1)
    coarse = assemble_rows(column_halo, count_x, count_y)
    flat_rows = coarse.reshape(count_x * count_y, 9)
    owners = owner[:, 0]
    strip_count = lax.axis_size("gx")
    capacity = max(2, 2 * count_x * count_y // strip_count)
    order_rank = ranks(owners)
    outgoing = (
        jnp.zeros((strip_count * capacity, 9), jnp.float32)
        .at[owners * capacity + order_rank]
        .set(flat_rows)
    )
    received = lax.all_to_all(outgoing, "gx", split_axis=0, concat_axis=0, tiled=True)
    return (current, received)


def solution(mesh):
    return jax.shard_map(
        local,
        mesh=mesh,
        in_specs=(
            P(None, "gx", "gy", None, None),
            P(None, None, "gx", "gy"),
            P(None, "gx", "gy"),
            P("gx", "gy", None, None),
            P("gx", "gy", None, None),
            P(None, "gx", "gy", None, None),
            P(("gx", "gy"), None),
        ),
        out_specs=(P(None, "gx", "gy", None, None), P(("gx", "gy"), None)),
        check_vma=False,
    )
```

profile of v0, /device:TPU:9, one launch (start us, length us, event | category | flops | bytes accessed | tf_op | source)
XLA Modules:
  0.0 330.9 jit_solution(14764148107720296920)
XLA Ops:
  1.5 3.9 %collective-permute-start = (f32[1,1,32,256]{3,2,1,0:T(8,128)S(1)}, f32[1,1,32,256]{3,2,1,0:T(8,128)S(1)}, u32[]{:S(2)}, u32[]{:S(2)}) collective-permute-start(f32[1,1,32,256]{3,2,1,0:T(8,128)S(1)} %get-tuple-element.99), channel_id=1, source_target_pairs={{0,16},{16,32},{32,48},{48,64},{64,80},{80,96},{96,112},{1,17},{17... | collective-permute-start | bytes 98312 | tf_op jit(solution)/shard_map/ppermute | solution.py:20
  6.7 4.9 %collective-permute-done.1 = f32[1,1,32,256]{3,2,1,0:T(8,128)S(1)} collective-permute-done((f32[1,1,32,256]{3,2,1,0:T(8,128)S(1)}, f32[1,1,32,256]{3,2,1,0:T(8,128)S(1)}, u32[]{:S(2)}, u32[]{:S(2)}) %collective-permute-start.1) | collective-permute-done | bytes 32800 | tf_op jit(solution)/shard_map/ppermute | solution.py:22
  13.3 6.3 %collective-permute-start.2 = (f32[1,1,320,32]{3,2,1,0:T(8,128)}, f32[1,1,320,32]{3,2,1,0:T(8,128)}, u32[]{:S(2)}, u32[]{:S(2)}) collective-permute-start(f32[1,1,320,32]{3,2,1,0:T(8,128)} %get-tuple-element.97), channel_id=1, source_target_pairs={{0,1},{1,2},{2,3},{3,4},{4,5},{5,6},{6,7},{7,8},{8,9},{9,10},{10,1... | collective-permute-start | bytes 122888 | tf_op jit(solution)/shard_map/ppermute | solution.py:20
  23.2 3.8 %collective-permute-start.4 = (f32[3,1,32,256]{3,2,1,0:T(8,128)}, f32[3,1,32,256]{3,2,1,0:T(8,128)}, u32[]{:S(2)}, u32[]{:S(2)}) collective-permute-start(f32[3,1,32,256]{3,2,1,0:T(8,128)} %get-tuple-element.66), channel_id=1, source_target_pairs={{0,16},{16,32},{32,48},{48,64},{64,80},{80,96},{96,112},{1,17},{17... | collective-permute-start | bytes 294920 | tf_op jit(solution)/shard_map/ppermute | solution.py:20
  39.2 5.4 %collective-permute-start.6 = (f32[3,1,320,32]{3,2,1,0:T(8,128)S(1)}, f32[3,1,320,32]{3,2,1,0:T(8,128)S(1)}, u32[]{:S(2)}, u32[]{:S(2)}) collective-permute-start(f32[3,1,320,32]{3,2,1,0:T(8,128)S(1)} %get-tuple-element.63), channel_id=1, source_target_pairs={{0,1},{1,2},{2,3},{3,4},{4,5},{5,6},{6,7},{7,8},{8,9},{9,10},{10,1... | collective-permute-start | bytes 368648 | tf_op jit(solution)/shard_map/ppermute | solution.py:20
  47.6 6.5 %collective-permute-done.6 = f32[3,1,320,32]{3,2,1,0:T(8,128)S(1)} collective-permute-done((f32[3,1,320,32]{3,2,1,0:T(8,128)S(1)}, f32[3,1,320,32]{3,2,1,0:T(8,128)S(1)}, u32[]{:S(2)}, u32[]{:S(2)}) %collective-permute-start.6) | collective-permute-done | bytes 122912 | tf_op jit(solution)/shard_map/ppermute | solution.py:20
  54.1 2.4 collective-permute-done.7
  57.1 2.2 reshape.73
  59.3 6.1 %fusion.51 = (f32[3,1,4,64,5,64]{5,4,3,2,0,1:T(8,128)}, f32[3,1,4,64,5,64]{5,4,3,2,0,1:T(8,128)}) fusion(f32[3,1,5,64,5,64]{5,4,3,2,0,1:T(8,128)} %reshape.73), kind=kLoop, calls=%fused_computation.157 | loop fusion | bytes 3932160 | tf_op jit(solution)/shard_map/slice | solution.py:32
  65.5 2.2 copy.123
  67.7 3.9 %copy.124 = f32[3,1,4,64,5,64]{3,5,4,2,1,0:T(8,128)} copy(f32[3,1,4,64,5,64]{5,4,3,2,0,1:T(8,128)} %get-tuple-element.40) | data formatting | bytes 1966080 | tf_op jit(solution)/shard_map/slice | solution.py:32
  73.6 2.0 fusion.1
  79.6 2.8 subtract_multiply_fusion.8
  84.5 2.7 copy.131
  87.2 2.3 reshape.74
  90.3 5.8 %collective-permute-start.8 = (f32[1,32,320]{2,1,0:T(8,128)S(1)}, f32[1,32,320]{2,1,0:T(8,128)S(1)}, u32[]{:S(2)}, u32[]{:S(2)}) collective-permute-start(f32[1,32,320]{2,1,0:T(8,128)S(1)} %get-tuple-element.90), channel_id=1, source_target_pairs={{0,16},{16,32},{32,48},{48,64},{64,80},{80,96},{96,112},{1,17},{17... | collective-permute-start | bytes 122888 | tf_op jit(solution)/shard_map/ppermute | solution.py:20
  98.5 4.2 %collective-permute-done.9 = f32[1,32,320]{2,1,0:T(8,128)S(1)} collective-permute-done((f32[1,32,320]{2,1,0:T(8,128)S(1)}, f32[1,32,320]{2,1,0:T(8,128)S(1)}, u32[]{:S(2)}, u32[]{:S(2)}) %collective-permute-start.9) | collective-permute-done | bytes 40992 | tf_op jit(solution)/shard_map/ppermute | solution.py:22
  102.8 4.1 %collective-permute-start.10 = (f32[1,384,32]{2,1,0:T(8,128)S(1)}, f32[1,384,32]{2,1,0:T(8,128)S(1)}, u32[]{:S(2)}, u32[]{:S(2)}) collective-permute-start(f32[1,384,32]{2,1,0:T(8,128)S(1)} %get-tuple-element.71), channel_id=1, source_target_pairs={{0,1},{1,2},{2,3},{3,4},{4,5},{5,6},{6,7},{7,8},{8,9},{9,10},{10,1... | collective-permute-start | bytes 147464 | tf_op jit(solution)/shard_map/ppermute | solution.py:20
  109.5 5.3 %collective-permute-done.11 = f32[1,384,32]{2,1,0:T(8,128)S(1)} collective-permute-done((f32[1,384,32]{2,1,0:T(8,128)S(1)}, f32[1,384,32]{2,1,0:T(8,128)S(1)}, u32[]{:S(2)}, u32[]{:S(2)}) %collective-permute-start.11) | collective-permute-done | bytes 49184 | tf_op jit(solution)/shard_map/ppermute | solution.py:22
  115.7 5.6 %collective-permute-start.12 = (f32[1,32,256]{2,1,0:T(8,128)S(1)}, f32[1,32,256]{2,1,0:T(8,128)S(1)}, u32[]{:S(2)}, u32[]{:S(2)}) collective-permute-start(f32[1,32,256]{2,1,0:T(8,128)S(1)} %get-tuple-element.85), channel_id=1, source_target_pairs={{0,16},{16,32},{32,48},{48,64},{64,80},{80,96},{96,112},{1,17},{17... | collective-permute-start | bytes 98312 | tf_op jit(solution)/shard_map/ppermute | solution.py:20
  122.7 4.7 %collective-permute-done.13 = f32[1,32,256]{2,1,0:T(8,128)S(1)} collective-permute-done((f32[1,32,256]{2,1,0:T(8,128)S(1)}, f32[1,32,256]{2,1,0:T(8,128)S(1)}, u32[]{:S(2)}, u32[]{:S(2)}) %collective-permute-start.13) | collective-permute-done | bytes 32800 | tf_op jit(solution)/shard_map/ppermute | solution.py:22
  127.6 3.8 %collective-permute-start.14 = (f32[1,320,32]{2,1,0:T(8,128)S(1)}, f32[1,320,32]{2,1,0:T(8,128)S(1)}, u32[]{:S(2)}, u32[]{:S(2)}) collective-permute-start(f32[1,320,32]{2,1,0:T(8,128)S(1)} %get-tuple-element.95), channel_id=1, source_target_pairs={{0,1},{1,2},{2,3},{3,4},{4,5},{5,6},{6,7},{7,8},{8,9},{9,10},{10,1... | collective-permute-start | bytes 122888 | tf_op jit(solution)/shard_map/ppermute | solution.py:20
  131.3 2.1 collective-permute-start.15
  134.6 4.2 %collective-permute-done.15 = f32[1,320,32]{2,1,0:T(8,128)S(1)} collective-permute-done((f32[1,320,32]{2,1,0:T(8,128)S(1)}, f32[1,320,32]{2,1,0:T(8,128)S(1)}, u32[]{:S(2)}, u32[]{:S(2)}) %collective-permute-start.15) | collective-permute-done | bytes 40992 | tf_op jit(solution)/shard_map/ppermute | solution.py:22
  139.9 2.3 reshape.75
  142.3 3.0 fusion.54
  145.3 2.3 copy.132
  147.6 2.3 copy.133
  159.0 2.7 copy.134
  161.7 2.3 reshape.76
  164.9 2.3 collective-permute-start.16
  169.5 4.5 %collective-permute-done.17 = f32[1,32,320]{2,1,0:T(8,128)S(1)} collective-permute-done((f32[1,32,320]{2,1,0:T(8,128)S(1)}, f32[1,32,320]{2,1,0:T(8,128)S(1)}, u32[]{:S(2)}, u32[]{:S(2)}) %collective-permute-start.17) | collective-permute-done | bytes 40992 | tf_op jit(solution)/shard_map/ppermute | solution.py:22
  174.2 3.2 collective-permute-start.18
  180.8 4.5 %collective-permute-done.19 = f32[1,384,32]{2,1,0:T(8,128)S(1)} collective-permute-done((f32[1,384,32]{2,1,0:T(8,128)S(1)}, f32[1,384,32]{2,1,0:T(8,128)S(1)}, u32[]{:S(2)}, u32[]{:S(2)}) %collective-permute-start.19) | collective-permute-done | bytes 49184 | tf_op jit(solution)/shard_map/ppermute | solution.py:22
  186.1 5.1 %collective-permute-start.20 = (f32[1,32,256]{2,1,0:T(8,128)S(1)}, f32[1,32,256]{2,1,0:T(8,128)S(1)}, u32[]{:S(2)}, u32[]{:S(2)}) collective-permute-start(f32[1,32,256]{2,1,0:T(8,128)S(1)} %get-tuple-element.79), channel_id=1, source_target_pairs={{0,16},{16,32},{32,48},{48,64},{64,80},{80,96},{96,112},{1,17},{17... | collective-permute-start | bytes 98312 | tf_op jit(solution)/shard_map/ppermute | solution.py:20
  192.7 4.7 %collective-permute-done.21 = f32[1,32,256]{2,1,0:T(8,128)S(1)} collective-permute-done((f32[1,32,256]{2,1,0:T(8,128)S(1)}, f32[1,32,256]{2,1,0:T(8,128)S(1)}, u32[]{:S(2)}, u32[]{:S(2)}) %collective-permute-start.21) | collective-permute-done | bytes 32800 | tf_op jit(solution)/shard_map/ppermute | solution.py:22
  197.6 3.8 %collective-permute-start.22 = (f32[1,320,32]{2,1,0:T(8,128)S(1)}, f32[1,320,32]{2,1,0:T(8,128)S(1)}, u32[]{:S(2)}, u32[]{:S(2)}) collective-permute-start(f32[1,320,32]{2,1,0:T(8,128)S(1)} %get-tuple-element.93), channel_id=1, source_target_pairs={{0,1},{1,2},{2,3},{3,4},{4,5},{5,6},{6,7},{7,8},{8,9},{9,10},{10,1... | collective-permute-start | bytes 122888 | tf_op jit(solution)/shard_map/ppermute | solution.py:20
  204.6 4.2 %collective-permute-done.23 = f32[1,320,32]{2,1,0:T(8,128)S(1)} collective-permute-done((f32[1,320,32]{2,1,0:T(8,128)S(1)}, f32[1,320,32]{2,1,0:T(8,128)S(1)}, u32[]{:S(2)}, u32[]{:S(2)}) %collective-permute-start.23) | collective-permute-done | bytes 40992 | tf_op jit(solution)/shard_map/ppermute | solution.py:22
  209.9 2.3 reshape.77
  212.3 3.0 fusion.53
  215.3 2.3 copy.135
  217.6 2.3 copy.136
  229.0 2.7 copy.137
  231.7 2.3 reshape.78
  239.2 4.5 %collective-permute-done.25 = f32[1,32,320]{2,1,0:T(8,128)S(1)} collective-permute-done((f32[1,32,320]{2,1,0:T(8,128)S(1)}, f32[1,32,320]{2,1,0:T(8,128)S(1)}, u32[]{:S(2)}, u32[]{:S(2)}) %collective-permute-start.25) | collective-permute-done | bytes 40992 | tf_op jit(solution)/shard_map/ppermute | solution.py:22
  243.8 3.2 collective-permute-start.26
  247.1 2.1 collective-permute-start.27
  250.4 4.5 %collective-permute-done.27 = f32[1,384,32]{2,1,0:T(8,128)S(1)} collective-permute-done((f32[1,384,32]{2,1,0:T(8,128)S(1)}, f32[1,384,32]{2,1,0:T(8,128)S(1)}, u32[]{:S(2)}, u32[]{:S(2)}) %collective-permute-start.27) | collective-permute-done | bytes 49184 | tf_op jit(solution)/shard_map/ppermute | solution.py:22
  255.8 5.1 %collective-permute-start.28 = (f32[1,32,256]{2,1,0:T(8,128)S(1)}, f32[1,32,256]{2,1,0:T(8,128)S(1)}, u32[]{:S(2)}, u32[]{:S(2)}) collective-permute-start(f32[1,32,256]{2,1,0:T(8,128)S(1)} %get-tuple-element.73), channel_id=1, source_target_pairs={{0,16},{16,32},{32,48},{48,64},{64,80},{80,96},{96,112},{1,17},{17... | collective-permute-start | bytes 98312 | tf_op jit(solution)/shard_map/ppermute | solution.py:20
  262.4 4.7 %collective-permute-done.29 = f32[1,32,256]{2,1,0:T(8,128)S(1)} collective-permute-done((f32[1,32,256]{2,1,0:T(8,128)S(1)}, f32[1,32,256]{2,1,0:T(8,128)S(1)}, u32[]{:S(2)}, u32[]{:S(2)}) %collective-permute-start.29) | collective-permute-done | bytes 32800 | tf_op jit(solution)/shard_map/ppermute | solution.py:22
  267.9 3.8 %collective-permute-start.30 = (f32[1,320,32]{2,1,0:T(8,128)}, f32[1,320,32]{2,1,0:T(8,128)}, u32[]{:S(2)}, u32[]{:S(2)}) collective-permute-start(f32[1,320,32]{2,1,0:T(8,128)} %get-tuple-element.91), channel_id=1, source_target_pairs={{0,1},{1,2},{2,3},{3,4},{4,5},{5,6},{6,7},{7,8},{8,9},{9,10},{10,1... | collective-permute-start | bytes 122888 | tf_op jit(solution)/shard_map/ppermute | solution.py:20
  273.8 2.6 copy.140
  276.4 3.2 collective-permute-done.31
  281.6 2.3 reshape.79
  283.9 3.0 fusion.52
  287.0 2.3 copy.138
  289.3 2.3 copy.139
  297.1 2.5 fusion.28
  304.0 4.5 %collective-permute-done.33 = f32[9,1,4]{0,2,1:T(4,128)S(1)} collective-permute-done((f32[9,1,4]{0,2,1:T(4,128)S(1)}, f32[9,1,4]{0,2,1:T(4,128)S(1)}, u32[]{:S(2)}, u32[]{:S(2)}) %collective-permute-start.33) | collective-permute-done | bytes 176 | tf_op jit(solution)/shard_map/ppermute | solution.py:22
  308.8 3.8 %collective-permute-start.34 = (f32[9,6,1]{0,2,1:T(1,128)S(1)}, f32[9,6,1]{0,2,1:T(1,128)S(1)}, u32[]{:S(2)}, u32[]{:S(2)}) collective-permute-start(f32[9,6,1]{0,2,1:T(1,128)S(1)} %get-tuple-element.104), channel_id=1, source_target_pairs={{0,1},{1,2},{2,3},{3,4},{4,5},{5,6},{6,7},{7,8},{8,9},{9,10},{10,1... | collective-permute-start | bytes 656 | tf_op jit(solution)/shard_map/ppermute | solution.py:20
  314.7 3.7 %collective-permute-done.35 = f32[9,6,1]{0,2,1:T(1,128)S(1)} collective-permute-done((f32[9,6,1]{0,2,1:T(1,128)S(1)}, f32[9,6,1]{0,2,1:T(1,128)S(1)}, u32[]{:S(2)}, u32[]{:S(2)}) %collective-permute-start.35) | collective-permute-done | bytes 248 | tf_op jit(solution)/shard_map/ppermute | solution.py:22
  320.4 3.3 %all-to-all-start = ((f32[8,4,9]{2,1,0:T(4,128)}), f32[8,4,9]{2,1,0:T(4,128)S(1)}, u32[]{:S(2)}, u32[]{:S(2)}) async-start(f32[8,4,9]{2,1,0:T(4,128)} %bitcast.28), calls=%async_computation | async-start | bytes 32768 | tf_op jit(solution)/shard_map/all_to_all | solution.py:174
  323.8 2.5 copy.159
  326.3 3.9 %all-to-all-done = f32[8,4,9]{2,1,0:T(4,128)S(1)} async-done(((f32[8,4,9]{2,1,0:T(4,128)}), f32[8,4,9]{2,1,0:T(4,128)S(1)}, u32[]{:S(2)}, u32[]{:S(2)}) %all-to-all-start) | async-done | bytes 1184 | tf_op jit(solution)/shard_map/all_to_all | solution.py:174
  (228 shorter events, 101.5 us)
Async XLA Ops:
  0.6 27.7 %copy-start.32 = (f32[1,4,4,128,128]{4,3,2,1,0:T(8,128)S(1)}, f32[1,4,4,128,128]{4,3,2,1,0:T(8,128)}, u32[]{:S(2)}) copy-start(f32[1,4,4,128,128]{4,3,2,1,0:T(8,128)} %param.7) | copy-start | bytes 3145732
  1.5 5.2 %collective-permute-start = (f32[1,1,32,256]{3,2,1,0:T(8,128)S(1)}, f32[1,1,32,256]{3,2,1,0:T(8,128)S(1)}, u32[]{:S(2)}, u32[]{:S(2)}) collective-permute-start(f32[1,1,32,256]{3,2,1,0:T(8,128)S(1)} %get-tuple-element.99), channel_id=1, source_target_pairs={{0,16},{16,32},{32,48},{48,64},{64,80},{80,96},{96,112},{1,17},{17... | collective-permute-start | bytes 98312 | tf_op jit(solution)/shard_map/ppermute | solution.py:20
  5.4 6.2 %collective-permute-start.1 = (f32[1,1,32,256]{3,2,1,0:T(8,128)S(1)}, f32[1,1,32,256]{3,2,1,0:T(8,128)S(1)}, u32[]{:S(2)}, u32[]{:S(2)}) collective-permute-start(f32[1,1,32,256]{3,2,1,0:T(8,128)S(1)} %get-tuple-element.100), channel_id=1, source_target_pairs={{16,0},{32,16},{48,32},{64,48},{80,64},{96,80},{112,96},{17,1},{33... | collective-permute-start | bytes 98312 | tf_op jit(solution)/shard_map/ppermute | solution.py:22
  13.3 20.4 %collective-permute-start.2 = (f32[1,1,320,32]{3,2,1,0:T(8,128)}, f32[1,1,320,32]{3,2,1,0:T(8,128)}, u32[]{:S(2)}, u32[]{:S(2)}) collective-permute-start(f32[1,1,320,32]{3,2,1,0:T(8,128)} %get-tuple-element.97), channel_id=1, source_target_pairs={{0,1},{1,2},{2,3},{3,4},{4,5},{5,6},{6,7},{7,8},{8,9},{9,10},{10,1... | collective-permute-start | bytes 122888 | tf_op jit(solution)/shard_map/ppermute | solution.py:20
  19.7 14.1 %collective-permute-start.3 = (f32[1,1,320,32]{3,2,1,0:T(8,128)}, f32[1,1,320,32]{3,2,1,0:T(8,128)}, u32[]{:S(2)}, u32[]{:S(2)}) collective-permute-start(f32[1,1,320,32]{3,2,1,0:T(8,128)} %get-tuple-element.98), channel_id=1, source_target_pairs={{1,0},{2,1},{3,2},{4,3},{5,4},{6,5},{7,6},{8,7},{9,8},{10,9},{11,1... | collective-permute-start | bytes 122888 | tf_op jit(solution)/shard_map/ppermute | solution.py:22
  23.2 12.7 %collective-permute-start.4 = (f32[3,1,32,256]{3,2,1,0:T(8,128)}, f32[3,1,32,256]{3,2,1,0:T(8,128)}, u32[]{:S(2)}, u32[]{:S(2)}) collective-permute-start(f32[3,1,32,256]{3,2,1,0:T(8,128)} %get-tuple-element.66), channel_id=1, source_target_pairs={{0,16},{16,32},{32,48},{48,64},{64,80},{80,96},{96,112},{1,17},{17... | collective-permute-start | bytes 294920 | tf_op jit(solution)/shard_map/ppermute | solution.py:20
  27.0 11.1 %collective-permute-start.5 = (f32[3,1,32,256]{3,2,1,0:T(8,128)}, f32[3,1,32,256]{3,2,1,0:T(8,128)}, u32[]{:S(2)}, u32[]{:S(2)}) collective-permute-start(f32[3,1,32,256]{3,2,1,0:T(8,128)} %get-tuple-element.65), channel_id=1, source_target_pairs={{16,0},{32,16},{48,32},{64,48},{80,64},{96,80},{112,96},{17,1},{33... | collective-permute-start | bytes 294920 | tf_op jit(solution)/shard_map/ppermute | solution.py:22
  28.7 2.4 copy-start.5
  28.7 2.4 copy-start.33
  30.0 2.4 copy-start.34
  31.1 2.7 copy-start.31
  35.6 11.0 %copy-start.20 = (f32[1,1,4,64,5,64]{3,5,4,2,1,0:T(8,128)}, f32[1,1,4,64,5,64]{3,5,4,2,1,0:T(8,128)S(1)}, u32[]{:S(2)}) copy-start(f32[1,1,4,64,5,64]{3,5,4,2,1,0:T(8,128)S(1)} %copy.120) | copy-start | bytes 983044
  35.9 10.7 %copy-start.22 = (f32[1,1,4,64,5,64]{3,5,4,2,1,0:T(8,128)}, f32[1,1,4,64,5,64]{3,5,4,2,1,0:T(8,128)S(1)}, u32[]{:S(2)}) copy-start(f32[1,1,4,64,5,64]{3,5,4,2,1,0:T(8,128)S(1)} %copy.121) | copy-start | bytes 983044
  39.2 14.8 %collective-permute-start.6 = (f32[3,1,320,32]{3,2,1,0:T(8,128)S(1)}, f32[3,1,320,32]{3,2,1,0:T(8,128)S(1)}, u32[]{:S(2)}, u32[]{:S(2)}) collective-permute-start(f32[3,1,320,32]{3,2,1,0:T(8,128)S(1)} %get-tuple-element.63), channel_id=1, source_target_pairs={{0,1},{1,2},{2,3},{3,4},{4,5},{5,6},{6,7},{7,8},{8,9},{9,10},{10,1... | collective-permute-start | bytes 368648 | tf_op jit(solution)/shard_map/ppermute | solution.py:20
  44.7 11.9 %collective-permute-start.7 = (f32[3,1,320,32]{3,2,1,0:T(8,128)S(1)}, f32[3,1,320,32]{3,2,1,0:T(8,128)S(1)}, u32[]{:S(2)}, u32[]{:S(2)}) collective-permute-start(f32[3,1,320,32]{3,2,1,0:T(8,128)S(1)} %get-tuple-element.64), channel_id=1, source_target_pairs={{1,0},{2,1},{3,2},{4,3},{5,4},{6,5},{7,6},{8,7},{9,8},{10,9},{11,1... | collective-permute-start | bytes 368648 | tf_op jit(solution)/shard_map/ppermute | solution.py:22
  67.7 3.9 %copy-start.7 = (f32[3,1,4,64,5,64]{3,5,4,2,1,0:T(8,128)}, f32[3,1,4,64,5,64]{3,5,4,2,1,0:T(8,128)S(1)}, u32[]{:S(2)}) copy-start(f32[3,1,4,64,5,64]{3,5,4,2,1,0:T(8,128)S(1)} %copy.123) | copy-start | bytes 2949124
  71.6 2.0 copy-start.8
  75.7 1.5 copy-start.27
  75.7 1.8 copy-start.28
  77.6 1.5 copy-start.12
  77.6 1.7 copy-start.21
  77.6 1.9 copy-start.23
  77.6 2.1 copy-start.30
  90.3 7.1 %collective-permute-start.8 = (f32[1,32,320]{2,1,0:T(8,128)S(1)}, f32[1,32,320]{2,1,0:T(8,128)S(1)}, u32[]{:S(2)}, u32[]{:S(2)}) collective-permute-start(f32[1,32,320]{2,1,0:T(8,128)S(1)} %get-tuple-element.90), channel_id=1, source_target_pairs={{0,16},{16,32},{32,48},{48,64},{64,80},{80,96},{96,112},{1,17},{17... | collective-permute-start | bytes 122888 | tf_op jit(solution)/shard_map/ppermute | solution.py:20
  96.1 6.6 %collective-permute-start.9 = (f32[1,32,320]{2,1,0:T(8,128)S(1)}, f32[1,32,320]{2,1,0:T(8,128)S(1)}, u32[]{:S(2)}, u32[]{:S(2)}) collective-permute-start(f32[1,32,320]{2,1,0:T(8,128)S(1)} %get-tuple-element.89), channel_id=1, source_target_pairs={{16,0},{32,16},{48,32},{64,48},{80,64},{96,80},{112,96},{17,1},{33... | collective-permute-start | bytes 122888 | tf_op jit(solution)/shard_map/ppermute | solution.py:22
  102.8 6.7 %collective-permute-start.10 = (f32[1,384,32]{2,1,0:T(8,128)S(1)}, f32[1,384,32]{2,1,0:T(8,128)S(1)}, u32[]{:S(2)}, u32[]{:S(2)}) collective-permute-start(f32[1,384,32]{2,1,0:T(8,128)S(1)} %get-tuple-element.71), channel_id=1, source_target_pairs={{0,1},{1,2},{2,3},{3,4},{4,5},{5,6},{6,7},{7,8},{8,9},{9,10},{10,1... | collective-permute-start | bytes 147464 | tf_op jit(solution)/shard_map/ppermute | solution.py:20
  106.9 7.9 %collective-permute-start.11 = (f32[1,384,32]{2,1,0:T(8,128)S(1)}, f32[1,384,32]{2,1,0:T(8,128)S(1)}, u32[]{:S(2)}, u32[]{:S(2)}) collective-permute-start(f32[1,384,32]{2,1,0:T(8,128)S(1)} %get-tuple-element.72), channel_id=1, source_target_pairs={{1,0},{2,1},{3,2},{4,3},{5,4},{6,5},{7,6},{8,7},{9,8},{10,9},{11,1... | collective-permute-start | bytes 147464 | tf_op jit(solution)/shard_map/ppermute | solution.py:22
  115.7 7.0 %collective-permute-start.12 = (f32[1,32,256]{2,1,0:T(8,128)S(1)}, f32[1,32,256]{2,1,0:T(8,128)S(1)}, u32[]{:S(2)}, u32[]{:S(2)}) collective-permute-start(f32[1,32,256]{2,1,0:T(8,128)S(1)} %get-tuple-element.85), channel_id=1, source_target_pairs={{0,16},{16,32},{32,48},{48,64},{64,80},{80,96},{96,112},{1,17},{17... | collective-permute-start | bytes 98312 | tf_op jit(solution)/shard_map/ppermute | solution.py:20
  121.3 6.2 %collective-permute-start.13 = (f32[1,32,256]{2,1,0:T(8,128)S(1)}, f32[1,32,256]{2,1,0:T(8,128)S(1)}, u32[]{:S(2)}, u32[]{:S(2)}) collective-permute-start(f32[1,32,256]{2,1,0:T(8,128)S(1)} %get-tuple-element.86), channel_id=1, source_target_pairs={{16,0},{32,16},{48,32},{64,48},{80,64},{96,80},{112,96},{17,1},{33... | collective-permute-start | bytes 98312 | tf_op jit(solution)/shard_map/ppermute | solution.py:22
  127.6 7.1 %collective-permute-start.14 = (f32[1,320,32]{2,1,0:T(8,128)S(1)}, f32[1,320,32]{2,1,0:T(8,128)S(1)}, u32[]{:S(2)}, u32[]{:S(2)}) collective-permute-start(f32[1,320,32]{2,1,0:T(8,128)S(1)} %get-tuple-element.95), channel_id=1, source_target_pairs={{0,1},{1,2},{2,3},{3,4},{4,5},{5,6},{6,7},{7,8},{8,9},{9,10},{10,1... | collective-permute-start | bytes 122888 | tf_op jit(solution)/shard_map/ppermute | solution.py:20
  131.3 7.5 %collective-permute-start.15 = (f32[1,320,32]{2,1,0:T(8,128)S(1)}, f32[1,320,32]{2,1,0:T(8,128)S(1)}, u32[]{:S(2)}, u32[]{:S(2)}) collective-permute-start(f32[1,320,32]{2,1,0:T(8,128)S(1)} %get-tuple-element.96), channel_id=1, source_target_pairs={{1,0},{2,1},{3,2},{4,3},{5,4},{6,5},{7,6},{8,7},{9,8},{10,9},{11,1... | collective-permute-start | bytes 122888 | tf_op jit(solution)/shard_map/ppermute | solution.py:22
  149.9 1.5 copy-start.1
  149.9 1.7 copy-start.24
  153.8 1.5 copy-start.15
  153.8 1.8 copy-start.18
  164.9 3.6 %collective-permute-start.16 = (f32[1,32,320]{2,1,0:T(8,128)S(1)}, f32[1,32,320]{2,1,0:T(8,128)S(1)}, u32[]{:S(2)}, u32[]{:S(2)}) collective-permute-start(f32[1,32,320]{2,1,0:T(8,128)S(1)} %get-tuple-element.84), channel_id=1, source_target_pairs={{0,16},{16,32},{32,48},{48,64},{64,80},{80,96},{96,112},{1,17},{17... | collective-permute-start | bytes 122888 | tf_op jit(solution)/shard_map/ppermute | solution.py:20
  167.2 6.9 %collective-permute-start.17 = (f32[1,32,320]{2,1,0:T(8,128)S(1)}, f32[1,32,320]{2,1,0:T(8,128)S(1)}, u32[]{:S(2)}, u32[]{:S(2)}) collective-permute-start(f32[1,32,320]{2,1,0:T(8,128)S(1)} %get-tuple-element.83), channel_id=1, source_target_pairs={{16,0},{32,16},{48,32},{64,48},{80,64},{96,80},{112,96},{17,1},{33... | collective-permute-start | bytes 122888 | tf_op jit(solution)/shard_map/ppermute | solution.py:22
  174.2 6.6 %collective-permute-start.18 = (f32[1,384,32]{2,1,0:T(8,128)S(1)}, f32[1,384,32]{2,1,0:T(8,128)S(1)}, u32[]{:S(2)}, u32[]{:S(2)}) collective-permute-start(f32[1,384,32]{2,1,0:T(8,128)S(1)} %get-tuple-element.69), channel_id=1, source_target_pairs={{0,1},{1,2},{2,3},{3,4},{4,5},{5,6},{6,7},{7,8},{8,9},{9,10},{10,1... | collective-permute-start | bytes 147464 | tf_op jit(solution)/shard_map/ppermute | solution.py:20
  177.4 7.9 %collective-permute-start.19 = (f32[1,384,32]{2,1,0:T(8,128)S(1)}, f32[1,384,32]{2,1,0:T(8,128)S(1)}, u32[]{:S(2)}, u32[]{:S(2)}) collective-permute-start(f32[1,384,32]{2,1,0:T(8,128)S(1)} %get-tuple-element.70), channel_id=1, source_target_pairs={{1,0},{2,1},{3,2},{4,3},{5,4},{6,5},{7,6},{8,7},{9,8},{10,9},{11,1... | collective-permute-start | bytes 147464 | tf_op jit(solution)/shard_map/ppermute | solution.py:22
  186.1 6.6 %collective-permute-start.20 = (f32[1,32,256]{2,1,0:T(8,128)S(1)}, f32[1,32,256]{2,1,0:T(8,128)S(1)}, u32[]{:S(2)}, u32[]{:S(2)}) collective-permute-start(f32[1,32,256]{2,1,0:T(8,128)S(1)} %get-tuple-element.79), channel_id=1, source_target_pairs={{0,16},{16,32},{32,48},{48,64},{64,80},{80,96},{96,112},{1,17},{17... | collective-permute-start | bytes 98312 | tf_op jit(solution)/shard_map/ppermute | solution.py:20
  191.3 6.2 %collective-permute-start.21 = (f32[1,32,256]{2,1,0:T(8,128)S(1)}, f32[1,32,256]{2,1,0:T(8,128)S(1)}, u32[]{:S(2)}, u32[]{:S(2)}) collective-permute-start(f32[1,32,256]{2,1,0:T(8,128)S(1)} %get-tuple-element.80), channel_id=1, source_target_pairs={{16,0},{32,16},{48,32},{64,48},{80,64},{96,80},{112,96},{17,1},{33... | collective-permute-start | bytes 98312 | tf_op jit(solution)/shard_map/ppermute | solution.py:22
  197.6 7.1 %collective-permute-start.22 = (f32[1,320,32]{2,1,0:T(8,128)S(1)}, f32[1,320,32]{2,1,0:T(8,128)S(1)}, u32[]{:S(2)}, u32[]{:S(2)}) collective-permute-start(f32[1,320,32]{2,1,0:T(8,128)S(1)} %get-tuple-element.93), channel_id=1, source_target_pairs={{0,1},{1,2},{2,3},{3,4},{4,5},{5,6},{6,7},{7,8},{8,9},{9,10},{10,1... | collective-permute-start | bytes 122888 | tf_op jit(solution)/shard_map/ppermute | solution.py:20
  201.4 7.5 %collective-permute-start.23 = (f32[1,320,32]{2,1,0:T(8,128)S(1)}, f32[1,320,32]{2,1,0:T(8,128)S(1)}, u32[]{:S(2)}, u32[]{:S(2)}) collective-permute-start(f32[1,320,32]{2,1,0:T(8,128)S(1)} %get-tuple-element.94), channel_id=1, source_target_pairs={{1,0},{2,1},{3,2},{4,3},{5,4},{6,5},{7,6},{8,7},{9,8},{10,9},{11,1... | collective-permute-start | bytes 122888 | tf_op jit(solution)/shard_map/ppermute | solution.py:22
  219.9 1.5 copy-start.2
  219.9 1.7 copy-start.25
  223.8 1.5 copy-start.16
  223.9 1.8 copy-start.19
  234.8 3.3 collective-permute-start.24
  236.8 6.9 %collective-permute-start.25 = (f32[1,32,320]{2,1,0:T(8,128)S(1)}, f32[1,32,320]{2,1,0:T(8,128)S(1)}, u32[]{:S(2)}, u32[]{:S(2)}) collective-permute-start(f32[1,32,320]{2,1,0:T(8,128)S(1)} %get-tuple-element.77), channel_id=1, source_target_pairs={{16,0},{32,16},{48,32},{64,48},{80,64},{96,80},{112,96},{17,1},{33... | collective-permute-start | bytes 122888 | tf_op jit(solution)/shard_map/ppermute | solution.py:22
  243.8 6.6 %collective-permute-start.26 = (f32[1,384,32]{2,1,0:T(8,128)S(1)}, f32[1,384,32]{2,1,0:T(8,128)S(1)}, u32[]{:S(2)}, u32[]{:S(2)}) collective-permute-start(f32[1,384,32]{2,1,0:T(8,128)S(1)} %get-tuple-element.67), channel_id=1, source_target_pairs={{0,1},{1,2},{2,3},{3,4},{4,5},{5,6},{6,7},{7,8},{8,9},{9,10},{10,1... | collective-permute-start | bytes 147464 | tf_op jit(solution)/shard_map/ppermute | solution.py:20
  247.1 7.9 %collective-permute-start.27 = (f32[1,384,32]{2,1,0:T(8,128)S(1)}, f32[1,384,32]{2,1,0:T(8,128)S(1)}, u32[]{:S(2)}, u32[]{:S(2)}) collective-permute-start(f32[1,384,32]{2,1,0:T(8,128)S(1)} %get-tuple-element.68), channel_id=1, source_target_pairs={{1,0},{2,1},{3,2},{4,3},{5,4},{6,5},{7,6},{8,7},{9,8},{10,9},{11,1... | collective-permute-start | bytes 147464 | tf_op jit(solution)/shard_map/ppermute | solution.py:22
  255.3 18.3 %copy-start.35 = (s32[16,1]{0,1:T(1,128)S(1)}, s32[16,1]{0,1:T(1,128)}, u32[]{:S(2)}) copy-start(s32[16,1]{0,1:T(1,128)} %param.13) | copy-start | bytes 196
  255.8 6.6 %collective-permute-start.28 = (f32[1,32,256]{2,1,0:T(8,128)S(1)}, f32[1,32,256]{2,1,0:T(8,128)S(1)}, u32[]{:S(2)}, u32[]{:S(2)}) collective-permute-start(f32[1,32,256]{2,1,0:T(8,128)S(1)} %get-tuple-element.73), channel_id=1, source_target_pairs={{0,16},{16,32},{32,48},{48,64},{64,80},{80,96},{96,112},{1,17},{17... | collective-permute-start | bytes 98312 | tf_op jit(solution)/shard_map/ppermute | solution.py:20
  260.9 6.2 %collective-permute-start.29 = (f32[1,32,256]{2,1,0:T(8,128)S(1)}, f32[1,32,256]{2,1,0:T(8,128)S(1)}, u32[]{:S(2)}, u32[]{:S(2)}) collective-permute-start(f32[1,32,256]{2,1,0:T(8,128)S(1)} %get-tuple-element.74), channel_id=1, source_target_pairs={{16,0},{32,16},{48,32},{64,48},{80,64},{96,80},{112,96},{17,1},{33... | collective-permute-start | bytes 98312 | tf_op jit(solution)/shard_map/ppermute | solution.py:22
  267.9 8.5 %collective-permute-start.30 = (f32[1,320,32]{2,1,0:T(8,128)}, f32[1,320,32]{2,1,0:T(8,128)}, u32[]{:S(2)}, u32[]{:S(2)}) collective-permute-start(f32[1,320,32]{2,1,0:T(8,128)} %get-tuple-element.91), channel_id=1, source_target_pairs={{0,1},{1,2},{2,3},{3,4},{4,5},{5,6},{6,7},{7,8},{8,9},{9,10},{10,1... | collective-permute-start | bytes 122888 | tf_op jit(solution)/shard_map/ppermute | solution.py:20
  271.7 7.9 %collective-permute-start.31 = (f32[1,320,32]{2,1,0:T(8,128)}, f32[1,320,32]{2,1,0:T(8,128)}, u32[]{:S(2)}, u32[]{:S(2)}) collective-permute-start(f32[1,320,32]{2,1,0:T(8,128)} %get-tuple-element.92), channel_id=1, source_target_pairs={{1,0},{2,1},{3,2},{4,3},{5,4},{6,5},{7,6},{8,7},{9,8},{10,9},{11,1... | collective-permute-start | bytes 122888 | tf_op jit(solution)/shard_map/ppermute | solution.py:22
  291.6 1.5 copy-start.3
  291.6 1.7 copy-start.26
  295.6 1.5 copy-start.29
  300.7 3.3 collective-permute-start.32
  302.7 5.8 %collective-permute-start.33 = (f32[9,1,4]{0,2,1:T(4,128)S(1)}, f32[9,1,4]{0,2,1:T(4,128)S(1)}, u32[]{:S(2)}, u32[]{:S(2)}) collective-permute-start(f32[9,1,4]{0,2,1:T(4,128)S(1)} %get-tuple-element.106), channel_id=1, source_target_pairs={{16,0},{32,16},{48,32},{64,48},{80,64},{96,80},{112,96},{17,1},{33... | collective-permute-start | bytes 440 | tf_op jit(solution)/shard_map/ppermute | solution.py:22
  308.8 5.9 %collective-permute-start.34 = (f32[9,6,1]{0,2,1:T(1,128)S(1)}, f32[9,6,1]{0,2,1:T(1,128)S(1)}, u32[]{:S(2)}, u32[]{:S(2)}) collective-permute-start(f32[9,6,1]{0,2,1:T(1,128)S(1)} %get-tuple-element.104), channel_id=1, source_target_pairs={{0,1},{1,2},{2,3},{3,4},{4,5},{5,6},{6,7},{7,8},{8,9},{9,10},{10,1... | collective-permute-start | bytes 656 | tf_op jit(solution)/shard_map/ppermute | solution.py:20
  312.6 5.8 %collective-permute-start.35 = (f32[9,6,1]{0,2,1:T(1,128)S(1)}, f32[9,6,1]{0,2,1:T(1,128)S(1)}, u32[]{:S(2)}, u32[]{:S(2)}) collective-permute-start(f32[9,6,1]{0,2,1:T(1,128)S(1)} %get-tuple-element.103), channel_id=1, source_target_pairs={{1,0},{2,1},{3,2},{4,3},{5,4},{6,5},{7,6},{8,7},{9,8},{10,9},{11,1... | collective-permute-start | bytes 656 | tf_op jit(solution)/shard_map/ppermute | solution.py:22
  320.4 9.8 %all-to-all-start = ((f32[8,4,9]{2,1,0:T(4,128)}), f32[8,4,9]{2,1,0:T(4,128)S(1)}, u32[]{:S(2)}, u32[]{:S(2)}) async-start(f32[8,4,9]{2,1,0:T(4,128)} %bitcast.28), calls=%async_computation | async-start | bytes 32768 | tf_op jit(solution)/shard_map/all_to_all | solution.py:174
  (9 other events, 10.1 us)
where the time goes:
time: 335 us; the launch traced here: 331 us
  starting transfers between devices  106 us (32%)
  local copies, waits for them, and re-layouts  101 us (30%)
  waiting for transfers between devices  85.2 us (25%)
  other arithmetic  37.2 us (11%)
    ppermute x18, starting transfers between devices, with_halo(): lax.ppermute(tail, axis, [(i, (i + 1) % count) for i in range(ends)])  72.9 us
    ppermute x18, waiting for transfers between devices, with_halo(): lax.ppermute(head, axis, [((i + 1) % count, i) for i in range(ends)])  68.9 us
    ppermute x18, starting transfers between devices, with_halo(): lax.ppermute(head, axis, [((i + 1) % count, i) for i in range(ends)])  29.3 us
    slice x10, local copies, waits for them, and re-layouts, cut_windows(): pieces[..., :-1, :, :, :]  24.8 us
    unnamed x86, local copies, waits for them, and re-layouts  23.5 us
    ppermute x18, waiting for transfers between devices, with_halo(): lax.ppermute(tail, axis, [(i, (i + 1) % count) for i in range(ends)])  12.3 us
    slice x5, local copies, waits for them, and re-layouts, cut_windows(): pieces[..., 1:, :, :, :]  11.1 us
    reshape x5, local copies, waits for them, and re-layouts, cut_windows(): whole.reshape(leading + (count_x + 1, block_width, count_y + 1, block_wid...  9.44 us
  transfers between devices with their start and end apart: 37, of which 23 were waited for; matrix products, arithmetic and copies ran while one was open for 6% of the time, Pallas kernels for 0%

commit v1 on v0

v1 whole, which is shorter than its diff:
```python
import jax
import jax.numpy as jnp
from jax import lax
from jax.experimental import pallas as pl
from jax.experimental.pallas import tpu as pltpu
from jax.sharding import PartitionSpec as P

MESH = pl.DeviceIdType.MESH
OMEGA = 2.0 / 3.0
NGX, NGY = 8, 16
ROWS = 288
SLABS = 34
F32 = jnp.float32
YROWS = 608
P0 = 320


def lanes():
    return lax.broadcasted_iota(jnp.int32, (8, 128), 1)


def subs():
    return lax.broadcasted_iota(jnp.int32, (8, 128), 0)


def roll(x, shift):
    shift = shift % 128
    return x if shift == 0 else pltpu.roll(x, shift, 1)


def sroll(x, shift):
    shift = shift % 8
    return x if shift == 0 else pltpu.roll(x, shift, 0)


def flip(x):
    return pltpu.roll(x, 64, 1)


def fold_rows(parts):
    sub = subs()
    step = 1
    while len(parts) > 1:
        low = (sub // step) % 2 == 0
        merged = []
        for i in range(0, len(parts), 2):
            a, b = parts[i], parts[i + 1]
            merged.append(jnp.where(low, a, sroll(b, step)) + jnp.where(low, sroll(a, -step), b))
        parts = merged
        step *= 2
    return parts[0]


def kernel(
    basis, trans, reaction, support, codes, active, owner,
    out, rows_out,
    va, vb, sup, act, cod, tr, re, tx, ty, tyw, dg, kd, k4, ia, hc, ds, dsup,
    ys, yl, rs, rl, tb, cls, zz,
    lsem, ssem, rsem, s2, r2, st, rt,
):
    gx = lax.axis_index("gx")
    gy = lax.axis_index("gy")

    def exists(dx, dy):
        return (gx + dx >= 0) & (gx + dx < NGX) & (gy + dy >= 0) & (gy + dy < NGY)

    bar = pltpu.get_barrier_semaphore()
    peers = [(s, t) for t in (-1, 0, 1) for s in range(NGX) if (s, t) != (0, 0)]
    for s, t in peers:
        @pl.when(exists(0, t))
        def _(s=s, t=t):
            pl.semaphore_signal(bar, inc=1, device_id=((gx + s) % NGX, gy + t), device_id_type=MESH)

    loads = []

    def load(src, dst):
        c = pltpu.make_async_copy(src, dst, lsem.at[len(loads)])
        c.start()
        loads.append(c)

    wins = ((0, 24, 128, 0), (1, 0, 128, 1), (2, 0, 128, 0), (3, 0, 104, 1))
    for j, lo, hi, px in wins:
        at = 64 * j - 32 + lo + 16
        load(basis.at[j, :, pl.ds(lo, hi - lo), :], va.at[px, pl.ds(0, 4), pl.ds(at, hi - lo), :])
        load(support.at[j, :, pl.ds(lo, hi - lo), :], sup.at[px, :, pl.ds(at, hi - lo), :])
    for i, (j, lo) in enumerate(((0, 0), (3, 88))):
        load(basis.at[j, :, pl.ds(lo, 40), :], ds.at[i])
        load(support.at[j, :, pl.ds(lo, 40), :], dsup.at[i])
    load(trans, tr.at[:, pl.ds(16, 256), :])
    load(reaction, re.at[pl.ds(16, 256), :])
    n_first = len(loads)
    for j, lo, hi in ((0, 24, 128), (2, 0, 128), (3, 64, 104)):
        at = 64 * j - 32 + lo + 16
        load(active.at[j, :, pl.ds(lo, hi - lo), :], act.at[:, pl.ds(at, hi - lo), :])
        load(codes.at[j, :, pl.ds(lo, hi - lo), :], cod.at[:, pl.ds(at, hi - lo), :])

    zero = jnp.zeros((8, 128), F32)
    for buf in (va, vb):
        for px in range(2):
            for kt in range(5):
                buf[px, kt, 0:8, :] = zero
                buf[px, kt, 280:288, :] = zero
    for kt in range(5):
        tx[kt, 0:8, :] = zero

    for dx in (1, -1):
        @pl.when(jnp.logical_not(exists(-dx, 0)))
        def _(dx=dx):
            px, at, ring, j, lo = (1, 8, 8, 3, 0) if dx == 1 else (0, 240, 272, 0, 0)
            for kt in range(4):
                va[px, kt, at:at + 40, :] = jnp.zeros((40, 128), F32)
                sup[px, kt, at:at + 40, :] = jnp.zeros((40, 128), jnp.int32)
            for f in range(3):
                tr[f, ring:ring + 8, :] = jnp.zeros((8, 256), F32)
            re[ring:ring + 8, :] = jnp.zeros((8, 256), F32)
            jo, ro = (0, 0) if dx == 1 else (3, 96)
            for k in range(4):
                out[jo, k, ro:ro + 32, :] = jnp.zeros((32, 128), F32)
    for dy, side in ((1, 0), (-1, 1)):
        @pl.when(jnp.logical_not(exists(0, -dy)))
        def _(side=side, dy=dy):
            yl[side, 48:560, :] = jnp.zeros((512, 128), F32)
            rl[side, 8:120, :] = jnp.zeros((112, 128), F32)
            for s in range(NGX):
                tb[1 - dy, s] = jnp.zeros((16, 128), F32)
        for dx in (1, -1):
            @pl.when(jnp.logical_not(exists(-dx, -dy)))
            def _(side=side, dx=dx):
                at = 0 if dx == 1 else 560
                yl[side, at:at + 48, :] = jnp.zeros((48, 128), F32)
                at = 120 if dx == 1 else 0
                rl[side, at:at + 8, :] = jnp.zeros((8, 128), F32)

    n_peers = 7 + NGX * (jnp.where(exists(0, -1), 1, 0) + jnp.where(exists(0, 1), 1, 0))
    pl.semaphore_wait(bar, n_peers)

    def remote(dx, dy, src, dst, i):
        return pltpu.make_async_remote_copy(
            src, dst, ssem.at[i], rsem.at[i], device_id=(gx + dx, gy + dy), device_id_type=MESH
        )

    def x_copies(dx):
        if dx == 1:
            j, lo, px, at, src_ring, dst_ring, i = 3, 88, 1, 8, 248, 8, 0
        else:
            j, lo, px, at, src_ring, dst_ring, i = 0, 0, 0, 240, 0, 272, 4
        return [
            remote(dx, 0, basis.at[j, :, pl.ds(lo, 40), :], va.at[px, pl.ds(0, 4), pl.ds(at, 40), :], i),
            remote(dx, 0, support.at[j, :, pl.ds(lo, 40), :], sup.at[px, :, pl.ds(at, 40), :], i + 1),
            remote(dx, 0, trans.at[:, pl.ds(src_ring, 8), :], tr.at[:, pl.ds(dst_ring, 8), :], i + 2),
            remote(dx, 0, reaction.at[pl.ds(src_ring, 8), :], re.at[pl.ds(dst_ring, 8), :], i + 3),
        ]

    def y_copy(dx, dy):
        side = 0 if dy == 1 else 1
        at, n = {0: (48, 512), 1: (0, 48), -1: (560, 48)}[dx]
        i = 8 + {0: 0, 1: 1, -1: 2}[dx] * 2 + side
        return [remote(dx, dy, ys.at[side, pl.ds(at, n), :], yl.at[side, pl.ds(at, n), :], i)]

    sends = [((dx, 0), x_copies(dx)) for dx in (1, -1)]
    for (dx, dy), cs in sends:
        @pl.when(exists(dx, dy))
        def _(cs=cs):
            for c in cs:
                c.start()

    for c in loads[:n_first]:
        c.wait()
    lane = lanes()
    right = lane >= 64

    def combine(i, _):
        r = pl.ds(pl.multiple_of(i * 8, 8), 8)
        re[r, :] = re[r, :] + tr[2, r, :]
        return 0

    lax.fori_loop(2, 34, combine, 0)

    for dx, jj in ((1, 1), (-1, 0)):
        for dy, side, k in ((1, 0, 3), (-1, 1, 0)):
            base = 8 if dx == 1 else 560
            for s in range(5):
                b = ds[jj, k, s * 8:s * 8 + 8, :]
                p = flip(dsup[jj, k, s * 8:s * 8 + 8, :].astype(F32))
                ys[side, base + s * 8:base + s * 8 + 8, :] = (
                    jnp.where(right, b, p) if dy == 1 else jnp.where(right, p, b)
                )
            at = 264 if dx == 1 else 16
            cell = []
            for f in range(3):
                ref = (lambda a, b: tr[f, a, b]) if f < 2 else (lambda a, b: re[a, b])
                x = ref(slice(at, at + 8), slice(128, 256) if dy == 1 else slice(0, 128))
                cell.append(roll(x, (8 + 8 * f) if dy == 1 else 8 * f))
            m = jnp.where(lane < 8, cell[0], jnp.where(lane < 16, cell[1], cell[2]))
            cat = 0 if dx == 1 else 600
            ys[side, cat:cat + 8, :] = m
    for dy in (1, -1):
        for dx in (1, -1):
            sends.append(((dx, dy), y_copy(dx, dy)))
            @pl.when(exists(dx, dy))
            def _(c=sends[-1][1]):
                c[0].start()

    for dy, side, k in ((1, 0, 3), (-1, 1, 0)):
        def pack(i, _, dy=dy, side=side, k=k):
            for px in range(2):
                src = pl.multiple_of(i * 8 + (8 if px == 0 else 48), 8)
                dst = pl.multiple_of(i * 8 + (8 + P0 if px == 0 else 48), 8)
                b = va[px, k, pl.ds(src, 8), :]
                p = flip(sup[px, k, pl.ds(src, 8), :].astype(F32))
                ys[side, pl.ds(dst, 8), :] = jnp.where(right, b, p) if dy == 1 else jnp.where(right, p, b)
            return 0

        lax.fori_loop(0, 29, pack, 0)
        for f in range(3):
            for h in range(2):
                m = None
                for i in range(16):
                    at = 16 + h * 128 + i * 8
                    col = slice(128, 256) if dy == 1 else slice(0, 128)
                    x = tr[f, at:at + 8, col] if f < 2 else re[at:at + 8, col]
                    x = roll(x, (8 * i + 8) if dy == 1 else 8 * i)
                    m = x if m is None else jnp.where(lane < 8 * i, m, x)
                at = 280 + (f * 2 + h) * 8
                ys[side, at:at + 8, :] = m
        sends.append(((0, dy), y_copy(0, dy)))
        @pl.when(exists(0, dy))
        def _(c=sends[-1][1]):
            c[0].start()

    for c in loads[n_first:]:
        c.wait()

    sub = subs()
    block = jnp.where(
        (sub >= 1) & (sub <= 4) & (lane >= 16) & (lane < 80), (sub - 1) * 4 + lane // 16 - 1, -1
    )
    own_of = jnp.full((8, 128), -1, jnp.int32)
    for n in range(16):
        own_of = jnp.where(block == n, owner[n], own_of)
    place = jnp.zeros((8, 128), jnp.int32)
    for n in range(16):
        place = place + jnp.where((own_of == owner[n]) & (block > n), 1, 0)
    target = jnp.where(block >= 0, own_of * 4 + place, -1).astype(F32)

    for (dx, dy), cs in sends:
        @pl.when(exists(-dx, -dy))
        def _(cs=cs):
            for c in cs:
                c.wait_recv()
    for at in (8, 272):
        re[at:at + 8, :] = re[at:at + 8, :] + tr[2, at:at + 8, :]

    for side in range(2):
        to = 24 if side == 0 else 96
        for f in range(3):
            for s in range(SLABS):
                if s == 0 or s == SLABS - 1:
                    at = 0 if s == 0 else 600
                    x = roll(yl[side, at:at + 8, :], to - 8 * f)
                else:
                    h, i = divmod(s - 1, 16)
                    at = 280 + (f * 2 + h) * 8
                    x = roll(yl[side, at:at + 8, :], to - 8 * i)
                hc[side, f, s * 8:s * 8 + 8, :] = x

    def spread(t0, t1, left, rite):
        r0, l0, r1, l1 = roll(t0, 32), roll(t0, -32), roll(t1, 32), roll(t1, -32)
        k0 = jnp.where(lane < 24, 0.0, jnp.where(lane < 32, left, r0))
        k1 = jnp.where(lane < 96, l0, l1)
        k2 = jnp.where(lane < 32, r0, r1)
        k3 = jnp.where(lane < 96, l1, jnp.where(lane < 104, rite, 0.0))
        return [k0, k1, k2, k3, jnp.where(right, flip(k0), flip(k3))]

    def prepare(i, _):
        r = pl.ds(pl.multiple_of(i * 8 + 8, 8), 8)
        h = pl.ds(pl.multiple_of(i * 8, 8), 8)
        cx = spread(tr[0, r, 0:128], tr[0, r, 128:256], hc[0, 0, h, :], hc[1, 0, h, :])
        cy = spread(tr[1, r, 0:128], tr[1, r, 128:256], hc[0, 1, h, :], hc[1, 1, h, :])
        cr = spread(re[r, 0:128], re[r, 128:256], hc[0, 2, h, :], hc[1, 2, h, :])
        live = [act[k, r, :].astype(F32) for k in range(4)]
        live.append(jnp.where(right, flip(live[0]), flip(live[3])))
        for kt in range(5):
            tx[kt, r, :] = cx[kt]
            ty[kt, r, :] = cy[kt]
            w = pltpu.roll(cy[kt], 1, 1)
            tyw[kt, r, :] = w
            prev = tx[kt, pl.ds(i * 8 + 7, 8), :]
            d = cr[kt] + cx[kt] + prev + cy[kt] + w
            dg[kt, r, :] = d
            wd = OMEGA / jnp.maximum(d, 0.005)
            ia[kt, r, :] = 1.0 - live[kt]
            for px in range(2):
                if kt < 4:
                    kept = sup[px, kt, r, :].astype(F32) * live[kt]
                else:
                    yr = pl.ds(pl.multiple_of(i * 8 + 8 + (P0 if px == 0 else 0), 8), 8)
                    from_low, from_high = yl[0, yr, :], yl[1, yr, :]
                    va[px, 4, r, :] = jnp.where(right, from_low, from_high)
                    kept = flip(jnp.where(right, from_high, from_low)) * live[4]
                kd[px, kt, r, :] = wd * kept
        return 0

    lax.fori_loop(0, SLABS, prepare, 0)

    low_x, high_x = gx == 0, gx == NGX - 1
    low_y, high_y = gy == 0, gy == NGY - 1

    def classify(i, _):
        r = pl.ds(pl.multiple_of(i * 8 + 16, 8), 8)
        h = i // 4
        thx = jnp.where((h == 0) | (h == 3) | (h == 4), 3, 6)
        thx = jnp.where((h == 0) & low_x, 6, thx)
        thx = jnp.where((h == 7) & high_x, 3, thx)
        got = []
        for k in range(4):
            c = cod[k, r, :]
            cy = c - 3 * (jnp.where(c >= 3, 1, 0) + jnp.where(c >= 6, 1, 0))
            thl = jnp.where(low_y, 2, 1) if k == 0 else 1
            thr = jnp.where(high_y, 1, 2) if k == 3 else 2
            thy = jnp.where(right, thr, thl)
            v = jnp.where(c >= thx, 2, 0) + jnp.where(cy >= thy, 1, 0)
            got.append(jnp.where(act[k, r, :] > 0, v, 4))
        k4 = jnp.where(right, flip(got[0]), flip(got[3]))
        cls[0, r, :] = jnp.where(lane >= 32, got[0], 4)
        cls[1, r, :] = got[1]
        cls[2, r, :] = got[2]
        cls[3, r, :] = jnp.where(lane < 96, got[3], 4)
        cls[4, r, :] = jnp.where((lane < 32) | (lane >= 96), k4, 4)
        return 0

    lax.fori_loop(0, 32, classify, 0)

    def flux_sum(v, px, kt, i):
        r = pl.ds(pl.multiple_of(i * 8 + 8, 8), 8)
        mid = v[px, kt, r, :]
        up = v[px, kt, pl.ds(i * 8 + 9, 8), :]
        dn = v[px, kt, pl.ds(i * 8 + 7, 8), :]
        total = (
            tx[kt, r, :] * up
            + tx[kt, pl.ds(i * 8 + 7, 8), :] * dn
            + ty[kt, r, :] * pltpu.roll(mid, 127, 1)
            + tyw[kt, r, :] * pltpu.roll(mid, 1, 1)
        )
        return mid, total

    def sweep(src, dst):
        def body(i, _):
            r = pl.ds(pl.multiple_of(i * 8 + 8, 8), 8)
            raw = [[None] * 5 for _ in range(2)]
            for kt in range(5):
                for px in range(2):
                    mid, total = flux_sum(src, px, kt, i)
                    raw[px][kt] = (1.0 - OMEGA) * mid + kd[px, kt, r, :] * total
            both = [raw[0][kt] + raw[1][kt] for kt in range(5)]
            turned = [flip(b) for b in both]
            for kt in range(5):
                t = both[kt] + jnp.where(right, turned[(kt + 1) % 5], turned[(kt + 4) % 5])
                t = jnp.maximum(t + ia[kt, r, :], 1e-30)
                inv = 1.0 / t
                for px in range(2):
                    dst[px, kt, r, :] = raw[px][kt] * inv
            return 0

        lax.fori_loop(0, SLABS, body, 0)

    sweep(va, vb)
    sweep(vb, va)
    sweep(va, vb)
    fin = vb

    for side in range(2):
        def place_lanes(xs, side=side):
            m = None
            for g, x in enumerate(xs):
                x = roll(x, 32 * g if side == 0 else 32 * g + 32)
                m = x if m is None else jnp.where(lane < 32 * g, m, x)
            return m

        rs[side, 0:8, :] = place_lanes([fin[1, 4, 16 + 8 * g:24 + 8 * g, :] for g in range(4)])
        rs[side, 120:128, :] = place_lanes([fin[0, 4, 240 + 8 * g:248 + 8 * g, :] for g in range(4)])

        def pack_back(i, _, side=side, place_lanes=place_lanes):
            def at(px, first):
                return fin[px, 4, pl.ds(pl.multiple_of(first + i * 8, 8), 8), :]

            rs[side, pl.ds(pl.multiple_of(8 + i * 8, 8), 8), :] = place_lanes(
                [at(0, 16), at(0, 16 + 112), at(1, 48), at(1, 48 + 112)]
            )
            return 0

        lax.fori_loop(0, 14, pack_back, 0)

    def remote2(dx, dy, src, dst, i):
        return pltpu.make_async_remote_copy(
            src, dst, s2.at[i], r2.at[i], device_id=(gx + dx, gy + dy), device_id_type=MESH
        )

    backs = [
        ((-1, 0), remote2(-1, 0, fin.at[1, pl.ds(0, 4), pl.ds(16, 32), :], out.at[3, :, pl.ds(96, 32), :], 0)),
        ((1, 0), remote2(1, 0, fin.at[0, pl.ds(0, 4), pl.ds(240, 32), :], out.at[0, :, pl.ds(0, 32), :], 1)),
    ]
    for dx in (0, 1, -1):
        for dy, side in ((1, 0), (-1, 1)):
            at, n = {0: (8, 112), 1: (120, 8), -1: (0, 8)}[dx]
            i = 2 + {0: 0, 1: 1, -1: 2}[dx] * 2 + side
            backs.append(
                ((dx, dy), remote2(dx, dy, rs.at[side, pl.ds(at, n), :], rl.at[side, pl.ds(at, n), :], i))
            )
    for (dx, dy), c in backs:
        @pl.when(exists(dx, dy))
        def _(c=c):
            c.start()

    def image(h, _):
        for kt in range(5):
            acc = [None] * 8
            for s in range(4):
                i = h * 4 + s + 1
                r = pl.ds(pl.multiple_of(i * 8 + 8, 8), 8)
                c = cls[kt, r, :]
                pick = [c == q for q in range(4)]
                for px in range(2):
                    mid, total = flux_sum(fin, px, kt, i)
                    img = dg[kt, r, :] * mid - total
                    for q in range(4):
                        n = (q // 2) * 4 + px * 2 + q % 2
                        x = jnp.where(pick[q], img, 0.0)
                        acc[n] = x if acc[n] is None else acc[n] + x
            zz[h, kt] = fold_rows(acc)
        return 0

    lax.fori_loop(0, 8, image, 0)

    table = jnp.zeros((8, 128), F32)
    bit_x, odd, bit_y = sub // 4, (sub // 2) % 2, sub % 2
    for a in range(5):
        part = jnp.zeros((8, 128), F32)
        base_x = a
        if a == 0:
            base_x = jnp.where(low_x, 1, 0)
        if a == 4:
            base_x = jnp.where(high_x, 3, 4)
        window_x = a - (a + odd) % 2
        dxo = window_x - (base_x - 1 + bit_x)
        for kt in range(5):
            z = zz[0, kt] if a == 0 else (zz[7, kt] if a == 4 else zz[2 * a - 1, kt] + zz[2 * a, kt])
            for shift in (32, 16, 8, 4, 2, 1):
                z = z + roll(z, -shift)
            for half in range(2):
                if kt < 4:
                    b, window_y = kt + half, kt
                else:
                    b, window_y = (4, 4) if half == 0 else (0, -1)
                base_y = b
                if b == 0:
                    base_y = jnp.where(low_y, 1, 0)
                if b == 4:
                    base_y = jnp.where(high_y, 3, 4)
                dyo = window_y - (base_y - 1 + bit_y)
                to = (base_y + bit_y) * 16 + (dxo + 1) * 3 + dyo + 1
                value = jnp.broadcast_to(z[:, 64 * half:64 * half + 1], (8, 128))
                part = part + jnp.where(lane == to, value, 0.0)
        low = jnp.sum(part[0:4], axis=0, keepdims=True)
        high = jnp.sum(part[4:8], axis=0, keepdims=True)
        table = table + jnp.where(sub == base_x, low, 0.0) + jnp.where(sub == base_x + 1, high, 0.0)
    tb[1, gx, 0:8, :] = table * (1.0 / 64.0)
    tb[1, gx, 8:16, :] = target

    hops = []
    for n, (s, t) in enumerate(peers):
        hops.append((t, pltpu.make_async_remote_copy(
            tb.at[1, gx], tb.at[1 - t, gx], st.at[n], rt.at[n],
            device_id=((gx + s) % NGX, gy + t), device_id_type=MESH,
        )))
    for t, c in hops:
        @pl.when(exists(0, t))
        def _(c=c):
            c.start()

    def emit(i, _):
        def one(j, px, first, to):
            for k in range(4):
                out[j, k, pl.ds(pl.multiple_of(to + i * 8, 8), 8), :] = fin[
                    px, k, pl.ds(pl.multiple_of(first + i * 8, 8), 8), :
                ]

        one(0, 0, 16, 32)
        one(1, 1, 48, 0)
        one(2, 0, 112, 0)
        one(3, 1, 176, 0)
        return 0

    lax.fori_loop(0, 12, emit, 0)
    for i in range(12, 16):
        for k in range(4):
            out[1, k, i * 8:i * 8 + 8, :] = fin[1, k, 48 + i * 8:56 + i * 8, :]
            out[2, k, i * 8:i * 8 + 8, :] = fin[0, k, 112 + i * 8:120 + i * 8, :]

    for (dx, dy), c in backs:
        @pl.when(exists(-dx, -dy))
        def _(c=c):
            c.wait_recv()

    for side, k in ((0, 0), (1, 3)):
        def merge(j, at, src, g):
            x = rl[side, pl.ds(src, 8), :]
            x = roll(x, -32 * g if side == 0 else 96 - 32 * g)
            inside = lane < 32 if side == 0 else lane >= 96
            out[j, k, at:at + 8, :] = jnp.where(inside, x, out[j, k, at:at + 8, :])

        for g in range(4):
            merge(0, 8 * g, 120, g)
            merge(3, 96 + 8 * g, 0, g)
        for s in range(28):
            j, at = (0, 32 + 8 * s) if s < 12 else (2, 8 * (s - 12))
            merge(j, at, 8 + 8 * (s % 14), s // 14)
            j, at = (1, 8 * s) if s < 16 else (3, 8 * (s - 16))
            merge(j, at, 8 + 8 * (s % 14), 2 + s // 14)

    for t, c in hops:
        @pl.when(exists(0, -t))
        def _(c=c):
            c.wait_recv()

    joined = []
    for s in range(NGX):
        a = tb[1, s, 0:8, :]
        below = roll(tb[0, s, 0:8, :], -64)
        above = roll(tb[2, s, 0:8, :], 64)
        group = lane // 16
        joined.append(a + jnp.where(group == 1, below, 0.0) + jnp.where(group == 4, above, 0.0))
    for s in range(NGX):
        t = joined[s]
        if s > 0:
            t = t + jnp.where(sub == 1, sroll(joined[s - 1], -4), 0.0)
        if s < NGX - 1:
            t = t + jnp.where(sub == 4, sroll(joined[s + 1], 4), 0.0)
        goal = tb[1, s, 8:16, :]
        for q in range(4):
            mine = jnp.where(goal == (gx * 4 + q).astype(F32), t, 0.0)
            line = jnp.sum(mine, axis=0, keepdims=True)
            line = line + pltpu.roll(line, 96, 1)
            line = line + pltpu.roll(line, 112, 1)
            rows_out[s * 4 + q:s * 4 + q + 1, :] = line[:, 16:25]

    for (dx, dy), cs in sends:
        @pl.when(exists(dx, dy))
        def _(cs=cs):
            for c in cs:
                c.wait_send()
    for (dx, dy), c in backs:
        @pl.when(exists(dx, dy))
        def _(c=c):
            c.wait_send()
    for t, c in hops:
        @pl.when(exists(0, t))
        def _(c=c):
            c.wait_send()


def local(basis, trans, reaction, support, codes, active, owner):
    anywhere = pl.BlockSpec(memory_space=pl.ANY)
    vmem = pl.BlockSpec(memory_space=pltpu.VMEM)
    sem = pltpu.SemaphoreType.DMA
    smoothed, coarse = pl.pallas_call(
        kernel,
        name="smooth",
        out_shape=(
            jax.ShapeDtypeStruct((4, 4, 128, 128), F32),
            jax.ShapeDtypeStruct((32, 9), F32),
        ),
        in_specs=[anywhere] * 6 + [pl.BlockSpec(memory_space=pltpu.SMEM)],
        out_specs=(vmem, vmem),
        scratch_shapes=[
            pltpu.VMEM((2, 5, ROWS, 128), F32),
            pltpu.VMEM((2, 5, ROWS, 128), F32),
            pltpu.VMEM((2, 4, ROWS, 128), jnp.int32),
            pltpu.VMEM((4, ROWS, 128), jnp.int32),
            pltpu.VMEM((4, ROWS, 128), jnp.int32),
            pltpu.VMEM((3, ROWS, 256), F32),
            pltpu.VMEM((ROWS, 256), F32),
            pltpu.VMEM((5, ROWS, 128), F32),
            pltpu.VMEM((5, ROWS, 128), F32),
            pltpu.VMEM((5, ROWS, 128), F32),
            pltpu.VMEM((5, ROWS, 128), F32),
            pltpu.VMEM((2, 5, ROWS, 128), F32),
            pltpu.VMEM((8, 128), F32),
            pltpu.VMEM((5, ROWS, 128), F32),
            pltpu.VMEM((2, 3, 272, 128), F32),
            pltpu.VMEM((2, 4, 40, 128), F32),
            pltpu.VMEM((2, 4, 40, 128), jnp.int32),
            pltpu.VMEM((2, YROWS, 128), F32),
            pltpu.VMEM((2, YROWS, 128), F32),
            pltpu.VMEM((2, 128, 128), F32),
            pltpu.VMEM((2, 128, 128), F32),
            pltpu.VMEM((3, NGX, 16, 128), F32),
            pltpu.VMEM((5, ROWS, 128), jnp.int32),
            pltpu.VMEM((8, 5, 8, 128), F32),
            sem((32,)), sem((16,)), sem((16,)), sem((8,)), sem((8,)), sem((24,)), sem((24,)),
        ],
        compiler_params=pltpu.CompilerParams(
            collective_id=0, has_side_effects=True, vmem_limit_bytes=48 << 20
        ),
    )(basis[0], trans[:, 0], reaction[0], support, codes, active[0], owner.reshape(16))
    return smoothed[None], coarse


def solution(mesh):
    return jax.shard_map(
        local,
        mesh=mesh,
        in_specs=(
            P(None, "gx", "gy", None, None),
            P(None, None, "gx", "gy"),
            P(None, "gx", "gy"),
            P("gx", "gy", None, None),
            P("gx", "gy", None, None),
            P(None, "gx", "gy", None, None),
            P(("gx", "gy"), None),
        ),
        out_specs=(P(None, "gx", "gy", None, None), P(("gx", "gy"), None)),
        check_vma=False,
    )
```

time: 335 us -> 72.8 us (0.22); the launches traced: 331 us -> 72.5 us
  starting transfers between devices: 106 us -> 0 us
  local copies, waits for them, and re-layouts: 101 us -> 8.05 us
  waiting for transfers between devices: 85.2 us -> 0 us
  Pallas kernels: 0 us -> 63.8 us
  other arithmetic: 37.2 us -> 0 us
    ppermute x36 -> x0, starting transfers between devices: 102 us -> none  [the longest x18 72.9 us: with_halo(): lax.ppermute(tail, axis, [(i, (i + 1) % count) for i in range(ends)])]
    ppermute x36 -> x0, waiting for transfers between devices: 81.2 us -> none  [the longest x18 68.9 us: with_halo(): lax.ppermute(head, axis, [((i + 1) % count, i) for i in range(ends)])]
    pallas_call x0 -> x1, Pallas kernels: none -> 63.8 us  [local(): pl.pallas_call(kernel, name='smooth', out_shape=(jax.ShapeDtypeStruct((4,...]
    slice x50 -> x0, local copies, waits for them, and re-layouts: 49.1 us -> none  [the longest x10 24.8 us: cut_windows(): pieces[..., :-1, :, :, :]]
    reshape x8 -> x0, local copies, waits for them, and re-layouts: 16.4 us -> none  [the longest x5 9.44 us: cut_windows(): whole.reshape(leading + (count_x + 1, block_width, count_y + 1, block_wid...]
    unnamed x86 -> x14, local copies, waits for them, and re-layouts: 23.5 us -> 8.05 us
    concatenate x19 -> x0, other arithmetic: 15.4 us -> none  [the longest x14 7.79 us: with_halo(): jnp.concatenate([lax.ppermute(tail, axis, [(i, (i + 1) % count) for i in...]
    transpose x3 -> x0, local copies, waits for them, and re-layouts: 8 us -> none  [spread_windows(): summed = jnp.swapaxes(summed, -3, -2)]
  transfers between devices with their start and end apart: 37 -> 0, of which waited for: 23 -> 0; matrix products, arithmetic and copies ran while one was open for 6% -> 0% of each run, Pallas kernels for 0% -> 0%
where the time goes in v1:
time: 72.8 us; the launch traced here: 72.5 us
  Pallas kernels  63.8 us (88%)
  local copies, waits for them, and re-layouts  8.05 us (11%)
    pallas_call x1, Pallas kernels, local(): pl.pallas_call(kernel, name='smooth', out_shape=(jax.ShapeDtypeStruct((4,...  63.8 us
    unnamed x14, local copies, waits for them, and re-layouts  8.05 us

profile of v1, /device:TPU:9, one launch (start us, length us, event | category | flops | bytes accessed | tf_op | source)
XLA Modules:
  0.0 72.5 jit_solution(5663515127672272222)
XLA Ops:
  0.6 0.0 copy-start.5
  0.6 0.6 copy-done.5
  1.3 0.0 copy-start
  1.3 1.2 %copy-done = f32[1,4,4,128,128]{4,3,2,1,0:T(8,128)S(1)} copy-done((f32[1,4,4,128,128]{4,3,2,1,0:T(8,128)S(1)}, f32[1,4,4,128,128]{4,3,2,1,0:T(8,128)}, u32[]{:S(2)}) %copy-start) | copy-done | bytes 1048600
  2.5 0.0 copy-start.1
  2.5 1.2 %copy-done.1 = s32[4,4,128,128]{3,2,1,0:T(8,128)S(1)} copy-done((s32[4,4,128,128]{3,2,1,0:T(8,128)S(1)}, s32[4,4,128,128]{3,2,1,0:T(8,128)}, u32[]{:S(2)}) %copy-start.1) | copy-done | bytes 1048600
  3.7 0.0 copy-start.2
  3.7 1.2 %copy-done.2 = s32[4,4,128,128]{3,2,1,0:T(8,128)S(1)} copy-done((s32[4,4,128,128]{3,2,1,0:T(8,128)S(1)}, s32[4,4,128,128]{3,2,1,0:T(8,128)}, u32[]{:S(2)}) %copy-start.2) | copy-done | bytes 1048600
  5.0 0.0 copy-start.3
  5.0 1.1 %copy-done.3 = f32[3,1,256,256]{3,2,1,0:T(8,128)S(1)} copy-done((f32[3,1,256,256]{3,2,1,0:T(8,128)S(1)}, f32[3,1,256,256]{3,2,1,0:T(8,128)}, u32[]{:S(2)}) %copy-start.3) | copy-done | bytes 786456
  6.1 0.0 copy-start.4
  6.1 0.9 %copy-done.4 = f32[1,256,256]{2,1,0:T(8,128)S(1)} copy-done((f32[1,256,256]{2,1,0:T(8,128)S(1)}, f32[1,256,256]{2,1,0:T(8,128)}, u32[]{:S(2)}) %copy-start.4) | copy-done | bytes 262168
  7.0 63.8 %smooth.1 = (f32[4,4,128,128]{3,2,1,0:T(8,128)S(1)}, f32[32,9]{1,0:T(8,128)S(1)}) custom-call(f32[4,4,128,128]{3,2,1,0:T(8,128)S(1)} %bitcast.7, f32[3,256,256]{2,1,0:T(8,128)S(1)} %bitcast.8, f32[256,256]{1,0:T(8,128)S(1)} %bitcast.9, s32[4,4,128,128]{3,2,1,0:T(8,128)S(1)} %copy-done.1, s32[4,4,128,128]{3,2,1,0:T(8,128)S(1)} %copy-done.2, ...), custom_call_target="tpu_custom_call" | custom-call | tf_op jit(solution)/shard_map/smooth/pallas_call | solution.py:566
  70.9 0.7 copy.9
  71.6 1.0 %copy.11 = f32[1,4,4,128,128]{4,3,2,1,0:T(8,128)} copy(f32[1,4,4,128,128]{4,3,2,1,0:T(8,128)S(1)} %bitcast.6) | data formatting | bytes 2097152
Async XLA Ops:
  0.6 0.7 copy-start.5
  1.3 1.2 %copy-start = (f32[1,4,4,128,128]{4,3,2,1,0:T(8,128)S(1)}, f32[1,4,4,128,128]{4,3,2,1,0:T(8,128)}, u32[]{:S(2)}) copy-start(f32[1,4,4,128,128]{4,3,2,1,0:T(8,128)} %param.7) | copy-start | bytes 3145732
  2.5 1.2 %copy-start.1 = (s32[4,4,128,128]{3,2,1,0:T(8,128)S(1)}, s32[4,4,128,128]{3,2,1,0:T(8,128)}, u32[]{:S(2)}) copy-start(s32[4,4,128,128]{3,2,1,0:T(8,128)} %support.1) | copy-start | bytes 3145732
  3.7 1.2 %copy-start.2 = (s32[4,4,128,128]{3,2,1,0:T(8,128)S(1)}, s32[4,4,128,128]{3,2,1,0:T(8,128)}, u32[]{:S(2)}) copy-start(s32[4,4,128,128]{3,2,1,0:T(8,128)} %codes.1) | copy-start | bytes 3145732
  5.0 1.1 %copy-start.3 = (f32[3,1,256,256]{3,2,1,0:T(8,128)S(1)}, f32[3,1,256,256]{3,2,1,0:T(8,128)}, u32[]{:S(2)}) copy-start(f32[3,1,256,256]{3,2,1,0:T(8,128)} %param.8) | copy-start | bytes 2359300
  6.1 0.9 %copy-start.4 = (f32[1,256,256]{2,1,0:T(8,128)S(1)}, f32[1,256,256]{2,1,0:T(8,128)}, u32[]{:S(2)}) copy-start(f32[1,256,256]{2,1,0:T(8,128)} %param.9) | copy-start | bytes 786436

commit v2 on v1

--- a/solution.py
+++ b/solution.py
@@ -11,8 +11,8 @@
 ROWS = 288
 SLABS = 34
 F32 = jnp.float32
-YROWS = 608
-P0 = 320
+YROWS = 544
+CROWS = 64
 
 
 def lanes():
@@ -54,8 +54,8 @@
 def kernel(
     basis, trans, reaction, support, codes, active, owner,
     out, rows_out,
-    va, vb, sup, act, cod, tr, re, tx, ty, tyw, dg, kd, k4, ia, hc, ds, dsup,
-    ys, yl, rs, rl, tb, cls, zz,
+    va, vb, sup, act, cod, tr, re, tx, ty, tyw, dg, kd, ia, hc, ds, dsup,
+    ys, yl, yc, yd, rs, rl, tb, cls, zz,
     lsem, ssem, rsem, s2, r2, st, rt,
 ):
     gx = lax.axis_index("gx")
@@ -78,6 +78,9 @@
         c.start()
         loads.append(c)
 
+    load(trans, tr.at[:, pl.ds(16, 256), :])
+    load(reaction, re.at[pl.ds(16, 256), :])
+    n_coef = len(loads)
     wins = ((0, 24, 128, 0), (1, 0, 128, 1), (2, 0, 128, 0), (3, 0, 104, 1))
     for j, lo, hi, px in wins:
         at = 64 * j - 32 + lo + 16
@@ -86,8 +89,6 @@
     for i, (j, lo) in enumerate(((0, 0), (3, 88))):
         load(basis.at[j, :, pl.ds(lo, 40), :], ds.at[i])
         load(support.at[j, :, pl.ds(lo, 40), :], dsup.at[i])
-    load(trans, tr.at[:, pl.ds(16, 256), :])
-    load(reaction, re.at[pl.ds(16, 256), :])
     n_first = len(loads)
     for j, lo, hi in ((0, 24, 128), (2, 0, 128), (3, 64, 104)):
         at = 64 * j - 32 + lo + 16
@@ -119,17 +120,52 @@
     for dy, side in ((1, 0), (-1, 1)):
         @pl.when(jnp.logical_not(exists(0, -dy)))
         def _(side=side, dy=dy):
-            yl[side, 48:560, :] = jnp.zeros((512, 128), F32)
+            yl[side, 40:504, :] = jnp.zeros((464, 128), F32)
+            yd[side, 8:56, :] = jnp.zeros((48, 128), F32)
             rl[side, 8:120, :] = jnp.zeros((112, 128), F32)
             for s in range(NGX):
                 tb[1 - dy, s] = jnp.zeros((16, 128), F32)
         for dx in (1, -1):
             @pl.when(jnp.logical_not(exists(-dx, -dy)))
             def _(side=side, dx=dx):
-                at = 0 if dx == 1 else 560
-                yl[side, at:at + 48, :] = jnp.zeros((48, 128), F32)
+                at = 0 if dx == 1 else 504
+                yl[side, at:at + 40, :] = jnp.zeros((40, 128), F32)
+                at = 0 if dx == 1 else 56
+                yd[side, at:at + 8, :] = jnp.zeros((8, 128), F32)
                 at = 120 if dx == 1 else 0
                 rl[side, at:at + 8, :] = jnp.zeros((8, 128), F32)
+
+    lane = lanes()
+    sub = subs()
+    right = lane >= 64
+
+    for c in loads[:n_coef]:
+        c.wait()
+
+    def combine(i, _):
+        r = pl.ds(pl.multiple_of(i * 8, 8), 8)
+        re[r, :] = re[r, :] + tr[2, r, :]
+        return 0
+
+    lax.fori_loop(2, 34, combine, 0, unroll=8)
+
+    def cells(f, at, high):
+        col = slice(128, 256) if high else slice(0, 128)
+        return tr[f, at:at + 8, col] if f < 2 else re[at:at + 8, col]
+
+    for dy, side in ((1, 0), (-1, 1)):
+        high = dy == 1
+        for dx, at, to in ((1, 264, 0), (-1, 16, 56)):
+            got = [roll(cells(f, at, high), (8 + 8 * f) if high else 8 * f) for f in range(3)]
+            yc[side, to:to + 8, :] = jnp.where(lane < 8, got[0], jnp.where(lane < 16, got[1], got[2]))
+        for f in range(3):
+            for h in range(2):
+                m = None
+                for i in range(16):
+                    x = roll(cells(f, 16 + h * 128 + i * 8, high), (8 * i + 8) if high else 8 * i)
+                    m = x if m is None else jnp.where(lane < 8 * i, m, x)
+                to = 8 + (f * 2 + h) * 8
+                yc[side, to:to + 8, :] = m
 
     n_peers = 7 + NGX * (jnp.where(exists(0, -1), 1, 0) + jnp.where(exists(0, 1), 1, 0))
     pl.semaphore_wait(bar, n_peers)
@@ -139,99 +175,72 @@
             src, dst, ssem.at[i], rsem.at[i], device_id=(gx + dx, gy + dy), device_id_type=MESH
         )
 
-    def x_copies(dx):
-        if dx == 1:
-            j, lo, px, at, src_ring, dst_ring, i = 3, 88, 1, 8, 248, 8, 0
-        else:
-            j, lo, px, at, src_ring, dst_ring, i = 0, 0, 0, 240, 0, 272, 4
-        return [
+    def start(d, cs):
+        @pl.when(exists(*d))
+        def _():
+            for c in cs:
+                c.start()
+
+    coef_sends, sends = [], []
+    for dx in (1, -1):
+        src, dst, i = (248, 8, 0) if dx == 1 else (0, 272, 2)
+        coef_sends.append(((dx, 0), [
+            remote(dx, 0, trans.at[:, pl.ds(src, 8), :], tr.at[:, pl.ds(dst, 8), :], i),
+            remote(dx, 0, reaction.at[pl.ds(src, 8), :], re.at[pl.ds(dst, 8), :], i + 1),
+        ]))
+        start(*coef_sends[-1])
+    for dx in (0, 1, -1):
+        for dy, side in ((1, 0), (-1, 1)):
+            at, n = {0: (8, 48), 1: (0, 8), -1: (56, 8)}[dx]
+            i = 4 + {0: 0, 1: 1, -1: 2}[dx] * 2 + side
+            coef_sends.append(((dx, dy), [
+                remote(dx, dy, yc.at[side, pl.ds(at, n), :], yd.at[side, pl.ds(at, n), :], i)
+            ]))
+            start(*coef_sends[-1])
+    for dx in (1, -1):
+        j, lo, px, at, i = (3, 88, 1, 8, 10) if dx == 1 else (0, 0, 0, 240, 12)
+        sends.append(((dx, 0), [
             remote(dx, 0, basis.at[j, :, pl.ds(lo, 40), :], va.at[px, pl.ds(0, 4), pl.ds(at, 40), :], i),
             remote(dx, 0, support.at[j, :, pl.ds(lo, 40), :], sup.at[px, :, pl.ds(at, 40), :], i + 1),
-            remote(dx, 0, trans.at[:, pl.ds(src_ring, 8), :], tr.at[:, pl.ds(dst_ring, 8), :], i + 2),
-            remote(dx, 0, reaction.at[pl.ds(src_ring, 8), :], re.at[pl.ds(dst_ring, 8), :], i + 3),
-        ]
-
-    def y_copy(dx, dy):
-        side = 0 if dy == 1 else 1
-        at, n = {0: (48, 512), 1: (0, 48), -1: (560, 48)}[dx]
-        i = 8 + {0: 0, 1: 1, -1: 2}[dx] * 2 + side
-        return [remote(dx, dy, ys.at[side, pl.ds(at, n), :], yl.at[side, pl.ds(at, n), :], i)]
-
-    sends = [((dx, 0), x_copies(dx)) for dx in (1, -1)]
-    for (dx, dy), cs in sends:
-        @pl.when(exists(dx, dy))
-        def _(cs=cs):
-            for c in cs:
-                c.start()
-
-    for c in loads[:n_first]:
+        ]))
+        start(*sends[-1])
+
+    def y_send(dx, dy, side):
+        at, n = {0: (40, 464), 1: (0, 40), -1: (504, 40)}[dx]
+        i = 14 + {0: 0, 1: 1, -1: 2}[dx] * 2 + side
+        sends.append(((dx, dy), [
+            remote(dx, dy, ys.at[side, pl.ds(at, n), :], yl.at[side, pl.ds(at, n), :], i)
+        ]))
+        start(*sends[-1])
+
+    for c in loads[n_coef:n_first]:
         c.wait()
-    lane = lanes()
-    right = lane >= 64
-
-    def combine(i, _):
-        r = pl.ds(pl.multiple_of(i * 8, 8), 8)
-        re[r, :] = re[r, :] + tr[2, r, :]
-        return 0
-
-    lax.fori_loop(2, 34, combine, 0)
-
     for dx, jj in ((1, 1), (-1, 0)):
         for dy, side, k in ((1, 0, 3), (-1, 1, 0)):
-            base = 8 if dx == 1 else 560
-            for s in range(5):
-                b = ds[jj, k, s * 8:s * 8 + 8, :]
-                p = flip(dsup[jj, k, s * 8:s * 8 + 8, :].astype(F32))
-                ys[side, base + s * 8:base + s * 8 + 8, :] = (
+            base = 0 if dx == 1 else 504
+            for n in range(5):
+                b = ds[jj, k, n * 8:n * 8 + 8, :]
+                p = flip(dsup[jj, k, n * 8:n * 8 + 8, :].astype(F32))
+                ys[side, base + n * 8:base + n * 8 + 8, :] = (
                     jnp.where(right, b, p) if dy == 1 else jnp.where(right, p, b)
                 )
-            at = 264 if dx == 1 else 16
-            cell = []
-            for f in range(3):
-                ref = (lambda a, b: tr[f, a, b]) if f < 2 else (lambda a, b: re[a, b])
-                x = ref(slice(at, at + 8), slice(128, 256) if dy == 1 else slice(0, 128))
-                cell.append(roll(x, (8 + 8 * f) if dy == 1 else 8 * f))
-            m = jnp.where(lane < 8, cell[0], jnp.where(lane < 16, cell[1], cell[2]))
-            cat = 0 if dx == 1 else 600
-            ys[side, cat:cat + 8, :] = m
-    for dy in (1, -1):
-        for dx in (1, -1):
-            sends.append(((dx, dy), y_copy(dx, dy)))
-            @pl.when(exists(dx, dy))
-            def _(c=sends[-1][1]):
-                c[0].start()
-
+            y_send(dx, dy, side)
     for dy, side, k in ((1, 0, 3), (-1, 1, 0)):
         def pack(i, _, dy=dy, side=side, k=k):
             for px in range(2):
                 src = pl.multiple_of(i * 8 + (8 if px == 0 else 48), 8)
-                dst = pl.multiple_of(i * 8 + (8 + P0 if px == 0 else 48), 8)
+                dst = pl.multiple_of(i * 8 + (272 if px == 0 else 40), 8)
                 b = va[px, k, pl.ds(src, 8), :]
                 p = flip(sup[px, k, pl.ds(src, 8), :].astype(F32))
                 ys[side, pl.ds(dst, 8), :] = jnp.where(right, b, p) if dy == 1 else jnp.where(right, p, b)
             return 0
 
-        lax.fori_loop(0, 29, pack, 0)
-        for f in range(3):
-            for h in range(2):
-                m = None
-                for i in range(16):
-                    at = 16 + h * 128 + i * 8
-                    col = slice(128, 256) if dy == 1 else slice(0, 128)
-                    x = tr[f, at:at + 8, col] if f < 2 else re[at:at + 8, col]
-                    x = roll(x, (8 * i + 8) if dy == 1 else 8 * i)
-                    m = x if m is None else jnp.where(lane < 8 * i, m, x)
-                at = 280 + (f * 2 + h) * 8
-                ys[side, at:at + 8, :] = m
-        sends.append(((0, dy), y_copy(0, dy)))
-        @pl.when(exists(0, dy))
-        def _(c=sends[-1][1]):
-            c[0].start()
+        lax.fori_loop(0, 29, pack, 0, unroll=29)
+        y_send(0, dy, side)
 
     for c in loads[n_first:]:
         c.wait()
 
-    sub = subs()
     block = jnp.where(
         (sub >= 1) & (sub <= 4) & (lane >= 16) & (lane < 80), (sub - 1) * 4 + lane // 16 - 1, -1
     )
@@ -242,66 +251,6 @@
     for n in range(16):
         place = place + jnp.where((own_of == owner[n]) & (block > n), 1, 0)
     target = jnp.where(block >= 0, own_of * 4 + place, -1).astype(F32)
-
-    for (dx, dy), cs in sends:
-        @pl.when(exists(-dx, -dy))
-        def _(cs=cs):
-            for c in cs:
-                c.wait_recv()
-    for at in (8, 272):
-        re[at:at + 8, :] = re[at:at + 8, :] + tr[2, at:at + 8, :]
-
-    for side in range(2):
-        to = 24 if side == 0 else 96
-        for f in range(3):
-            for s in range(SLABS):
-                if s == 0 or s == SLABS - 1:
-                    at = 0 if s == 0 else 600
-                    x = roll(yl[side, at:at + 8, :], to - 8 * f)
-                else:
-                    h, i = divmod(s - 1, 16)
-                    at = 280 + (f * 2 + h) * 8
-                    x = roll(yl[side, at:at + 8, :], to - 8 * i)
-                hc[side, f, s * 8:s * 8 + 8, :] = x
-
-    def spread(t0, t1, left, rite):
-        r0, l0, r1, l1 = roll(t0, 32), roll(t0, -32), roll(t1, 32), roll(t1, -32)
-        k0 = jnp.where(lane < 24, 0.0, jnp.where(lane < 32, left, r0))
-        k1 = jnp.where(lane < 96, l0, l1)
-        k2 = jnp.where(lane < 32, r0, r1)
-        k3 = jnp.where(lane < 96, l1, jnp.where(lane < 104, rite, 0.0))
-        return [k0, k1, k2, k3, jnp.where(right, flip(k0), flip(k3))]
-
-    def prepare(i, _):
-        r = pl.ds(pl.multiple_of(i * 8 + 8, 8), 8)
-        h = pl.ds(pl.multiple_of(i * 8, 8), 8)
-        cx = spread(tr[0, r, 0:128], tr[0, r, 128:256], hc[0, 0, h, :], hc[1, 0, h, :])
-        cy = spread(tr[1, r, 0:128], tr[1, r, 128:256], hc[0, 1, h, :], hc[1, 1, h, :])
-        cr = spread(re[r, 0:128], re[r, 128:256], hc[0, 2, h, :], hc[1, 2, h, :])
-        live = [act[k, r, :].astype(F32) for k in range(4)]
-        live.append(jnp.where(right, flip(live[0]), flip(live[3])))
-        for kt in range(5):
-            tx[kt, r, :] = cx[kt]
-            ty[kt, r, :] = cy[kt]
-            w = pltpu.roll(cy[kt], 1, 1)
-            tyw[kt, r, :] = w
-            prev = tx[kt, pl.ds(i * 8 + 7, 8), :]
-            d = cr[kt] + cx[kt] + prev + cy[kt] + w
-            dg[kt, r, :] = d
-            wd = OMEGA / jnp.maximum(d, 0.005)
-            ia[kt, r, :] = 1.0 - live[kt]
-            for px in range(2):
-                if kt < 4:
-                    kept = sup[px, kt, r, :].astype(F32) * live[kt]
-                else:
-                    yr = pl.ds(pl.multiple_of(i * 8 + 8 + (P0 if px == 0 else 0), 8), 8)
-                    from_low, from_high = yl[0, yr, :], yl[1, yr, :]
-                    va[px, 4, r, :] = jnp.where(right, from_low, from_high)
-                    kept = flip(jnp.where(right, from_high, from_low)) * live[4]
-                kd[px, kt, r, :] = wd * kept
-        return 0
-
-    lax.fori_loop(0, SLABS, prepare, 0)
 
     low_x, high_x = gx == 0, gx == NGX - 1
     low_y, high_y = gy == 0, gy == NGY - 1
@@ -329,7 +278,100 @@
         cls[4, r, :] = jnp.where((lane < 32) | (lane >= 96), k4, 4)
         return 0
 
-    lax.fori_loop(0, 32, classify, 0)
+    lax.fori_loop(0, 32, classify, 0, unroll=4)
+
+    def arrived(copies):
+        for (dx, dy), cs in copies:
+            @pl.when(exists(-dx, -dy))
+            def _(cs=cs):
+                for c in cs:
+                    c.wait_recv()
+
+    arrived(coef_sends)
+    for at in (8, 272):
+        re[at:at + 8, :] = re[at:at + 8, :] + tr[2, at:at + 8, :]
+    for side in range(2):
+        to = 24 if side == 0 else 96
+        for f in range(3):
+            for n in range(SLABS):
+                if n == 0 or n == SLABS - 1:
+                    at = 0 if n == 0 else 56
+                    x = roll(yd[side, at:at + 8, :], to - 8 * f)
+                else:
+                    h, i = divmod(n - 1, 16)
+                    at = 8 + (f * 2 + h) * 8
+                    x = roll(yd[side, at:at + 8, :], to - 8 * i)
+                hc[side, f, n * 8:n * 8 + 8, :] = x
+
+    def spread(t0, t1, left, rite):
+        r0, l0, r1, l1 = roll(t0, 32), roll(t0, -32), roll(t1, 32), roll(t1, -32)
+        k0 = jnp.where(lane < 24, 0.0, jnp.where(lane < 32, left, r0))
+        k1 = jnp.where(lane < 96, l0, l1)
+        k2 = jnp.where(lane < 32, r0, r1)
+        k3 = jnp.where(lane < 96, l1, jnp.where(lane < 104, rite, 0.0))
+        return [k0, k1, k2, k3, jnp.where(right, flip(k0), flip(k3))]
+
+    def widen(i, _):
+        r = pl.ds(pl.multiple_of(i * 8 + 8, 8), 8)
+        h = pl.ds(pl.multiple_of(i * 8, 8), 8)
+        cx = spread(tr[0, r, 0:128], tr[0, r, 128:256], hc[0, 0, h, :], hc[1, 0, h, :])
+        cy = spread(tr[1, r, 0:128], tr[1, r, 128:256], hc[0, 1, h, :], hc[1, 1, h, :])
+        cr = spread(re[r, 0:128], re[r, 128:256], hc[0, 2, h, :], hc[1, 2, h, :])
+        live = [act[k, r, :].astype(F32) for k in range(4)]
+        live.append(jnp.where(right, flip(live[0]), flip(live[3])))
+        for kt in range(5):
+            tx[kt, r, :] = cx[kt]
+            ty[kt, r, :] = cy[kt]
+            dg[kt, r, :] = cr[kt]
+            ia[kt, r, :] = 1.0 - live[kt]
+        return 0
+
+    lax.fori_loop(0, SLABS, widen, 0, unroll=2)
+
+    def diagonal(i, _):
+        r = pl.ds(pl.multiple_of(i * 8 + 8, 8), 8)
+        for kt in range(5):
+            w = pltpu.roll(ty[kt, r, :], 1, 1)
+            tyw[kt, r, :] = w
+            d = dg[kt, r, :] + tx[kt, r, :] + tx[kt, pl.ds(i * 8 + 7, 8), :] + ty[kt, r, :] + w
+            dg[kt, r, :] = d
+            wd = OMEGA / jnp.maximum(d, 0.005)
+            if kt < 4:
+                wd = wd * (1.0 - ia[kt, r, :])
+            for px in range(2):
+                kd[px, kt, r, :] = wd
+        return 0
+
+    lax.fori_loop(0, SLABS, diagonal, 0, unroll=2)
+
+    def keep(first, px):
+        def body(i, _):
+            r = pl.ds(pl.multiple_of(i * 8 + first, 8), 8)
+            for k in range(4):
+                kd[px, k, r, :] = kd[px, k, r, :] * sup[px, k, r, :].astype(F32)
+            return 0
+
+        return body
+
+    lax.fori_loop(0, 29, keep(8, 0), 0, unroll=4)
+    lax.fori_loop(0, 29, keep(48, 1), 0, unroll=4)
+
+    arrived(sends)
+    lax.fori_loop(0, 5, keep(240, 0), 0, unroll=5)
+    lax.fori_loop(0, 5, keep(8, 1), 0, unroll=5)
+
+    def unpack(i, _):
+        r = pl.ds(pl.multiple_of(i * 8 + 8, 8), 8)
+        live = 1.0 - ia[4, r, :]
+        for px in range(2):
+            yr = pl.ds(pl.multiple_of(i * 8 + (272 if px == 0 else 0), 8), 8)
+            from_low, from_high = yl[0, yr, :], yl[1, yr, :]
+            va[px, 4, r, :] = jnp.where(right, from_low, from_high)
+            kept = flip(jnp.where(right, from_high, from_low)) * live
+            kd[px, 4, r, :] = kd[px, 4, r, :] * kept
+        return 0
+
+    lax.fori_loop(0, SLABS, unpack, 0, unroll=17)
 
     def flux_sum(v, px, kt, i):
         r = pl.ds(pl.multiple_of(i * 8 + 8, 8), 8)
@@ -345,30 +387,51 @@
         return mid, total
 
     def sweep(src, dst):
-        def body(i, _):
+        def first(i):
             r = pl.ds(pl.multiple_of(i * 8 + 8, 8), 8)
-            raw = [[None] * 5 for _ in range(2)]
+            raw = []
             for kt in range(5):
                 for px in range(2):
                     mid, total = flux_sum(src, px, kt, i)
-                    raw[px][kt] = (1.0 - OMEGA) * mid + kd[px, kt, r, :] * total
-            both = [raw[0][kt] + raw[1][kt] for kt in range(5)]
-            turned = [flip(b) for b in both]
+                    raw.append((1.0 - OMEGA) * mid + kd[px, kt, r, :] * total)
+            turned = [flip(raw[2 * kt] + raw[2 * kt + 1]) for kt in range(5)]
+            return tuple(raw), tuple(turned)
+
+        def second(i, raw, turned):
+            r = pl.ds(pl.multiple_of(i * 8 + 8, 8), 8)
             for kt in range(5):
-                t = both[kt] + jnp.where(right, turned[(kt + 1) % 5], turned[(kt + 4) % 5])
+                t = raw[2 * kt] + raw[2 * kt + 1]
+                t = t + jnp.where(right, turned[(kt + 1) % 5], turned[(kt + 4) % 5])
                 t = jnp.maximum(t + ia[kt, r, :], 1e-30)
-                inv = 1.0 / t
+                inv = pl.reciprocal(t, approx=True)
+                inv = inv * (2.0 - t * inv)
                 for px in range(2):
-                    dst[px, kt, r, :] = raw[px][kt] * inv
-            return 0
-
-        lax.fori_loop(0, SLABS, body, 0)
+                    dst[px, kt, r, :] = raw[2 * kt + px] * inv
+
+        def body(i, held):
+            new = first(i)
+            second(i - 1, *held)
+            return new
+
+        held = lax.fori_loop(1, SLABS, body, first(0), unroll=3)
+        second(SLABS - 1, *held)
 
     sweep(va, vb)
     sweep(vb, va)
     sweep(va, vb)
     fin = vb
 
+    def remote2(dx, dy, src, dst, i):
+        return pltpu.make_async_remote_copy(
+            src, dst, s2.at[i], r2.at[i], device_id=(gx + dx, gy + dy), device_id_type=MESH
+        )
+
+    backs = [
+        ((-1, 0), remote2(-1, 0, fin.at[1, pl.ds(0, 4), pl.ds(16, 32), :], out.at[3, :, pl.ds(96, 32), :], 0)),
+        ((1, 0), remote2(1, 0, fin.at[0, pl.ds(0, 4), pl.ds(240, 32), :], out.at[0, :, pl.ds(0, 32), :], 1)),
+    ]
+    for d, c in backs:
+        start(d, [c])
     for side in range(2):
         def place_lanes(xs, side=side):
             m = None
@@ -389,17 +452,8 @@
             )
             return 0
 
-        lax.fori_loop(0, 14, pack_back, 0)
-
-    def remote2(dx, dy, src, dst, i):
-        return pltpu.make_async_remote_copy(
-            src, dst, s2.at[i], r2.at[i], device_id=(gx + dx, gy + dy), device_id_type=MESH
-        )
-
-    backs = [
-        ((-1, 0), remote2(-1, 0, fin.at[1, pl.ds(0, 4), pl.ds(16, 32), :], out.at[3, :, pl.ds(96, 32), :], 0)),
-        ((1, 0), remote2(1, 0, fin.at[0, pl.ds(0, 4), pl.ds(240, 32), :], out.at[0, :, pl.ds(0, 32), :], 1)),
-    ]
+        lax.fori_loop(0, 14, pack_back, 0, unroll=14)
+
     for dx in (0, 1, -1):
         for dy, side in ((1, 0), (-1, 1)):
             at, n = {0: (8, 112), 1: (120, 8), -1: (0, 8)}[dx]
@@ -407,10 +461,7 @@
             backs.append(
                 ((dx, dy), remote2(dx, dy, rs.at[side, pl.ds(at, n), :], rl.at[side, pl.ds(at, n), :], i))
             )
-    for (dx, dy), c in backs:
-        @pl.when(exists(dx, dy))
-        def _(c=c):
-            c.start()
+            start((dx, dy), [backs[-1][1]])
 
     def image(h, _):
         for kt in range(5):
@@ -491,7 +542,7 @@
         one(3, 1, 176, 0)
         return 0
 
-    lax.fori_loop(0, 12, emit, 0)
+    lax.fori_loop(0, 12, emit, 0, unroll=4)
     for i in range(12, 16):
         for k in range(4):
             out[1, k, i * 8:i * 8 + 8, :] = fin[1, k, 48 + i * 8:56 + i * 8, :]
@@ -544,7 +595,7 @@
             line = line + pltpu.roll(line, 112, 1)
             rows_out[s * 4 + q:s * 4 + q + 1, :] = line[:, 16:25]
 
-    for (dx, dy), cs in sends:
+    for (dx, dy), cs in coef_sends + sends:
         @pl.when(exists(dx, dy))
         def _(cs=cs):
             for c in cs:
@@ -560,7 +611,7 @@
 
 
 def local(basis, trans, reaction, support, codes, active, owner):
-    anywhere = pl.BlockSpec(memory_space=pl.ANY)
+    anywhere = pl.BlockSpec(memory_space=pltpu.HBM)
     vmem = pl.BlockSpec(memory_space=pltpu.VMEM)
     sem = pltpu.SemaphoreType.DMA
     smoothed, coarse = pl.pallas_call(
@@ -585,22 +636,23 @@
             pltpu.VMEM((5, ROWS, 128), F32),
             pltpu.VMEM((5, ROWS, 128), F32),
             pltpu.VMEM((2, 5, ROWS, 128), F32),
-            pltpu.VMEM((8, 128), F32),
             pltpu.VMEM((5, ROWS, 128), F32),
             pltpu.VMEM((2, 3, 272, 128), F32),
             pltpu.VMEM((2, 4, 40, 128), F32),
             pltpu.VMEM((2, 4, 40, 128), jnp.int32),
             pltpu.VMEM((2, YROWS, 128), F32),
             pltpu.VMEM((2, YROWS, 128), F32),
+            pltpu.VMEM((2, CROWS, 128), F32),
+            pltpu.VMEM((2, CROWS, 128), F32),
             pltpu.VMEM((2, 128, 128), F32),
             pltpu.VMEM((2, 128, 128), F32),
             pltpu.VMEM((3, NGX, 16, 128), F32),
             pltpu.VMEM((5, ROWS, 128), jnp.int32),
             pltpu.VMEM((8, 5, 8, 128), F32),
-            sem((32,)), sem((16,)), sem((16,)), sem((8,)), sem((8,)), sem((24,)), sem((24,)),
+            sem((32,)), sem((24,)), sem((24,)), sem((8,)), sem((8,)), sem((24,)), sem((24,)),
         ],
         compiler_params=pltpu.CompilerParams(
-            collective_id=0, has_side_effects=True, vmem_limit_bytes=48 << 20
+            collective_id=0, has_side_effects=True, vmem_limit_bytes=60 << 20
         ),
     )(basis[0], trans[:, 0], reaction[0], support, codes, active[0], owner.reshape(16))
     return smoothed[None], coarse

time: 72.8 us -> 47.7 us (0.66)
  Pallas kernels: 63.8 us -> 43.1 us
  local copies, waits for them, and re-layouts: 8.05 us -> 3.69 us
    pallas_call x1, Pallas kernels: 63.8 us -> 43.1 us  [local(): pl.pallas_call(kernel, name='smooth', out_shape=(jax.ShapeDtypeStruct((4,...]
    unnamed x14 -> x2, local copies, waits for them, and re-layouts: 8.05 us -> 3.69 us
where the time goes in v2:
time: 47.7 us; the launch traced here: 47.5 us
  Pallas kernels  43.1 us (90%)
  local copies, waits for them, and re-layouts  3.69 us (8%)
  between operations  0.64 us (1%)
    pallas_call x1, Pallas kernels, local(): pl.pallas_call(kernel, name='smooth', out_shape=(jax.ShapeDtypeStruct((4,...  43.1 us
    unnamed x2, local copies, waits for them, and re-layouts  3.69 us

profile of v2, /device:TPU:9, one launch (start us, length us, event | category | flops | bytes accessed | tf_op | source)
XLA Modules:
  0.0 47.5 jit_solution(12786181040263757391)
XLA Ops:
  0.6 43.1 %smooth.1 = (f32[4,4,128,128]{3,2,1,0:T(8,128)}, f32[32,9]{1,0:T(8,128)}) custom-call(f32[4,4,128,128]{3,2,1,0:T(8,128)} %bitcast.7, f32[3,256,256]{2,1,0:T(8,128)} %bitcast.9, f32[256,256]{1,0:T(8,128)} %bitcast.10, s32[4,4,128,128]{3,2,1,0:T(8,128)} %support.1, s32[4,4,128,128]{3,2,1,0:T(8,128)} %codes.1, s32[4,4,128,128]{3,2,1,0:T(8,128)} %bitcast.8, ...), custom_call_target="tpu_custom_call" | custom-call | tf_op jit(solution)/shard_map/smooth/pallas_call | solution.py:617
  43.8 1.4 %copy.9 = f32[32,9]{0,1:T(8,128)} copy(f32[32,9]{1,0:T(8,128)} %get-tuple-element.7) | data formatting | bytes 2304
  45.2 2.3 %copy.11 = f32[1,4,4,128,128]{4,3,2,1,0:T(8,128)} copy(f32[1,4,4,128,128]{4,3,2,1,0:T(8,128)} %bitcast.6) | data formatting | bytes 2097152

commit v3 on v2

--- a/solution.py
+++ b/solution.py
@@ -11,7 +11,7 @@
 ROWS = 288
 SLABS = 34
 F32 = jnp.float32
-YROWS = 544
+YROWS = 392
 CROWS = 64
 
 
@@ -54,9 +54,9 @@
 def kernel(
     basis, trans, reaction, support, codes, active, owner,
     out, rows_out,
-    va, vb, sup, act, cod, tr, re, tx, ty, tyw, dg, kd, ia, hc, ds, dsup,
-    ys, yl, yc, yd, rs, rl, tb, cls, zz,
-    lsem, ssem, rsem, s2, r2, st, rt,
+    va, vb, sup, act, cod, tr, re, tx, ty, tyw, dg, kd, ia, ds, dsup,
+    ys, yl, yc, yd, rs, rl, tb, tg, cls, zz,
+    lsem, ssem, rsem, s2, r2, st, rt, sg, rg,
 ):
     gx = lax.axis_index("gx")
     gy = lax.axis_index("gy")
@@ -104,6 +104,11 @@
     for kt in range(5):
         tx[kt, 0:8, :] = zero
 
+    for kt in range(4):
+        va[1, kt, 8:12, :] = jnp.zeros((4, 128), F32)
+        va[0, kt, 276:280, :] = jnp.zeros((4, 128), F32)
+        sup[1, kt, 8:12, :] = jnp.zeros((4, 128), jnp.int32)
+        sup[0, kt, 276:280, :] = jnp.zeros((4, 128), jnp.int32)
     for dx in (1, -1):
         @pl.when(jnp.logical_not(exists(-dx, 0)))
         def _(dx=dx):
@@ -120,15 +125,15 @@
     for dy, side in ((1, 0), (-1, 1)):
         @pl.when(jnp.logical_not(exists(0, -dy)))
         def _(side=side, dy=dy):
-            yl[side, 40:504, :] = jnp.zeros((464, 128), F32)
+            yl[side, 40:352, :] = jnp.zeros((312, 128), F32)
             yd[side, 8:56, :] = jnp.zeros((48, 128), F32)
             rl[side, 8:120, :] = jnp.zeros((112, 128), F32)
             for s in range(NGX):
-                tb[1 - dy, s] = jnp.zeros((16, 128), F32)
+                tb[1 - dy, s] = jnp.zeros((8, 128), F32)
         for dx in (1, -1):
             @pl.when(jnp.logical_not(exists(-dx, -dy)))
             def _(side=side, dx=dx):
-                at = 0 if dx == 1 else 504
+                at = 0 if dx == 1 else 352
                 yl[side, at:at + 40, :] = jnp.zeros((40, 128), F32)
                 at = 0 if dx == 1 else 56
                 yd[side, at:at + 8, :] = jnp.zeros((8, 128), F32)
@@ -166,6 +171,54 @@
                     m = x if m is None else jnp.where(lane < 8 * i, m, x)
                 to = 8 + (f * 2 + h) * 8
                 yc[side, to:to + 8, :] = m
+
+    block = jnp.where(
+        (sub >= 1) & (sub <= 4) & (lane >= 16) & (lane < 80), (sub - 1) * 4 + lane // 16 - 1, -1
+    )
+    own_of = jnp.full((8, 128), -1, jnp.int32)
+    for n in range(16):
+        own_of = jnp.where(block == n, owner[n], own_of)
+    place = jnp.zeros((8, 128), jnp.int32)
+    for n in range(16):
+        place = place + jnp.where((own_of == owner[n]) & (block > n), 1, 0)
+    tg[gx] = jnp.where(block >= 0, own_of * 4 + place, -1).astype(F32)
+
+    for c in loads[n_coef:n_first]:
+        c.wait()
+
+    def chunks(xs, shift):
+        m = None
+        for n, x in enumerate(xs):
+            x = roll(x, shift + 40 * n)
+            m = x if m is None else jnp.where(lane < 40 * n, m, x)
+        return m
+
+    for dy, side, k, shift in ((1, 0, 3, -88), (-1, 1, 0, 0)):
+        def value(i, px, k=k):
+            return va[px, k, pl.ds(pl.multiple_of(i * 8 + (8 if px == 0 else 48), 8), 8), :]
+
+        def mask(i, px, k=k):
+            return sup[px, k, pl.ds(pl.multiple_of(i * 8 + (8 if px == 0 else 48), 8), 8), :].astype(F32)
+
+        def pack(i, _, side=side, shift=shift, value=value, mask=mask):
+            ys[side, pl.ds(pl.multiple_of(i * 8 + 40, 8), 8), :] = chunks(
+                [value(i, 0), value(i, 1), mask(i, 0)], shift
+            )
+            return 0
+
+        lax.fori_loop(0, 29, pack, 0, unroll=29)
+        for i in range(10):
+            ys[side, 272 + 8 * i:280 + 8 * i, :] = chunks(
+                [mask(min(i + 10 * n, 28), 1) for n in range(3)], shift
+            )
+        for dx, jj in ((1, 1), (-1, 0)):
+            base = 0 if dx == 1 else 352
+            for n in range(5):
+                b = ds[jj, k, n * 8:n * 8 + 8, :]
+                p = flip(dsup[jj, k, n * 8:n * 8 + 8, :].astype(F32))
+                ys[side, base + n * 8:base + n * 8 + 8, :] = (
+                    jnp.where(right, b, p) if dy == 1 else jnp.where(right, p, b)
+                )
 
     n_peers = 7 + NGX * (jnp.where(exists(0, -1), 1, 0) + jnp.where(exists(0, 1), 1, 0))
     pl.semaphore_wait(bar, n_peers)
@@ -197,60 +250,35 @@
                 remote(dx, dy, yc.at[side, pl.ds(at, n), :], yd.at[side, pl.ds(at, n), :], i)
             ]))
             start(*coef_sends[-1])
+    def y_send(dx, dy, side):
+        at, n = {0: (40, 312), 1: (0, 40), -1: (352, 40)}[dx]
+        i = 14 + {0: 0, 1: 1, -1: 2}[dx] * 2 + side
+        cs = [remote(dx, dy, ys.at[side, pl.ds(at, n), :], yl.at[side, pl.ds(at, n), :], i)]
+        (sends if dx else side_sends).append(((dx, dy), cs))
+        start((dx, dy), cs)
+
+    side_sends = []
+    y_send(0, 1, 0)
+    y_send(0, -1, 1)
     for dx in (1, -1):
-        j, lo, px, at, i = (3, 88, 1, 8, 10) if dx == 1 else (0, 0, 0, 240, 12)
+        j, lo, px, at, i = (3, 92, 1, 12, 10) if dx == 1 else (0, 0, 0, 240, 12)
         sends.append(((dx, 0), [
-            remote(dx, 0, basis.at[j, :, pl.ds(lo, 40), :], va.at[px, pl.ds(0, 4), pl.ds(at, 40), :], i),
-            remote(dx, 0, support.at[j, :, pl.ds(lo, 40), :], sup.at[px, :, pl.ds(at, 40), :], i + 1),
+            remote(dx, 0, basis.at[j, :, pl.ds(lo, 36), :], va.at[px, pl.ds(0, 4), pl.ds(at, 36), :], i),
+            remote(dx, 0, support.at[j, :, pl.ds(lo, 36), :], sup.at[px, :, pl.ds(at, 36), :], i + 1),
         ]))
         start(*sends[-1])
-
-    def y_send(dx, dy, side):
-        at, n = {0: (40, 464), 1: (0, 40), -1: (504, 40)}[dx]
-        i = 14 + {0: 0, 1: 1, -1: 2}[dx] * 2 + side
-        sends.append(((dx, dy), [
-            remote(dx, dy, ys.at[side, pl.ds(at, n), :], yl.at[side, pl.ds(at, n), :], i)
-        ]))
-        start(*sends[-1])
-
-    for c in loads[n_coef:n_first]:
-        c.wait()
-    for dx, jj in ((1, 1), (-1, 0)):
-        for dy, side, k in ((1, 0, 3), (-1, 1, 0)):
-            base = 0 if dx == 1 else 504
-            for n in range(5):
-                b = ds[jj, k, n * 8:n * 8 + 8, :]
-                p = flip(dsup[jj, k, n * 8:n * 8 + 8, :].astype(F32))
-                ys[side, base + n * 8:base + n * 8 + 8, :] = (
-                    jnp.where(right, b, p) if dy == 1 else jnp.where(right, p, b)
-                )
-            y_send(dx, dy, side)
-    for dy, side, k in ((1, 0, 3), (-1, 1, 0)):
-        def pack(i, _, dy=dy, side=side, k=k):
-            for px in range(2):
-                src = pl.multiple_of(i * 8 + (8 if px == 0 else 48), 8)
-                dst = pl.multiple_of(i * 8 + (272 if px == 0 else 40), 8)
-                b = va[px, k, pl.ds(src, 8), :]
-                p = flip(sup[px, k, pl.ds(src, 8), :].astype(F32))
-                ys[side, pl.ds(dst, 8), :] = jnp.where(right, b, p) if dy == 1 else jnp.where(right, p, b)
-            return 0
-
-        lax.fori_loop(0, 29, pack, 0, unroll=29)
-        y_send(0, dy, side)
+    for dx in (1, -1):
+        y_send(dx, 1, 0)
+        y_send(dx, -1, 1)
+    goals = []
+    for n in range(1, NGX):
+        goals.append(pltpu.make_async_remote_copy(
+            tg.at[gx], tg.at[gx], sg.at[n], rg.at[n],
+            device_id=((gx + n) % NGX, gy), device_id_type=MESH,
+        ))
 
     for c in loads[n_first:]:
         c.wait()
-
-    block = jnp.where(
-        (sub >= 1) & (sub <= 4) & (lane >= 16) & (lane < 80), (sub - 1) * 4 + lane // 16 - 1, -1
-    )
-    own_of = jnp.full((8, 128), -1, jnp.int32)
-    for n in range(16):
-        own_of = jnp.where(block == n, owner[n], own_of)
-    place = jnp.zeros((8, 128), jnp.int32)
-    for n in range(16):
-        place = place + jnp.where((own_of == owner[n]) & (block > n), 1, 0)
-    target = jnp.where(block >= 0, own_of * 4 + place, -1).astype(F32)
 
     low_x, high_x = gx == 0, gx == NGX - 1
     low_y, high_y = gy == 0, gy == NGY - 1
@@ -287,62 +315,86 @@
                 for c in cs:
                     c.wait_recv()
 
-    arrived(coef_sends)
-    for at in (8, 272):
-        re[at:at + 8, :] = re[at:at + 8, :] + tr[2, at:at + 8, :]
-    for side in range(2):
-        to = 24 if side == 0 else 96
-        for f in range(3):
-            for n in range(SLABS):
-                if n == 0 or n == SLABS - 1:
-                    at = 0 if n == 0 else 56
-                    x = roll(yd[side, at:at + 8, :], to - 8 * f)
-                else:
-                    h, i = divmod(n - 1, 16)
-                    at = 8 + (f * 2 + h) * 8
-                    x = roll(yd[side, at:at + 8, :], to - 8 * i)
-                hc[side, f, n * 8:n * 8 + 8, :] = x
-
-    def spread(t0, t1, left, rite):
+    def spread(t0, t1):
         r0, l0, r1, l1 = roll(t0, 32), roll(t0, -32), roll(t1, 32), roll(t1, -32)
-        k0 = jnp.where(lane < 24, 0.0, jnp.where(lane < 32, left, r0))
+        k0 = jnp.where(lane < 32, 0.0, r0)
         k1 = jnp.where(lane < 96, l0, l1)
         k2 = jnp.where(lane < 32, r0, r1)
-        k3 = jnp.where(lane < 96, l1, jnp.where(lane < 104, rite, 0.0))
+        k3 = jnp.where(lane < 96, l1, 0.0)
         return [k0, k1, k2, k3, jnp.where(right, flip(k0), flip(k3))]
 
     def widen(i, _):
         r = pl.ds(pl.multiple_of(i * 8 + 8, 8), 8)
-        h = pl.ds(pl.multiple_of(i * 8, 8), 8)
-        cx = spread(tr[0, r, 0:128], tr[0, r, 128:256], hc[0, 0, h, :], hc[1, 0, h, :])
-        cy = spread(tr[1, r, 0:128], tr[1, r, 128:256], hc[0, 1, h, :], hc[1, 1, h, :])
-        cr = spread(re[r, 0:128], re[r, 128:256], hc[0, 2, h, :], hc[1, 2, h, :])
-        live = [act[k, r, :].astype(F32) for k in range(4)]
-        live.append(jnp.where(right, flip(live[0]), flip(live[3])))
+        cx = spread(tr[0, r, 0:128], tr[0, r, 128:256])
+        cy = spread(tr[1, r, 0:128], tr[1, r, 128:256])
+        cr = spread(re[r, 0:128], re[r, 128:256])
         for kt in range(5):
             tx[kt, r, :] = cx[kt]
             ty[kt, r, :] = cy[kt]
             dg[kt, r, :] = cr[kt]
+        return 0
+
+    def dead(i, _):
+        r = pl.ds(pl.multiple_of(i * 8 + 8, 8), 8)
+        live = [act[k, r, :].astype(F32) for k in range(4)]
+        live.append(jnp.where(right, flip(live[0]), flip(live[3])))
+        for kt in range(5):
             ia[kt, r, :] = 1.0 - live[kt]
         return 0
 
-    lax.fori_loop(0, SLABS, widen, 0, unroll=2)
-
-    def diagonal(i, _):
-        r = pl.ds(pl.multiple_of(i * 8 + 8, 8), 8)
-        for kt in range(5):
-            w = pltpu.roll(ty[kt, r, :], 1, 1)
-            tyw[kt, r, :] = w
-            d = dg[kt, r, :] + tx[kt, r, :] + tx[kt, pl.ds(i * 8 + 7, 8), :] + ty[kt, r, :] + w
-            dg[kt, r, :] = d
-            wd = OMEGA / jnp.maximum(d, 0.005)
-            if kt < 4:
-                wd = wd * (1.0 - ia[kt, r, :])
-            for px in range(2):
-                kd[px, kt, r, :] = wd
-        return 0
-
-    lax.fori_loop(0, SLABS, diagonal, 0, unroll=2)
+    def diagonal(lo, hi, kts, unroll):
+        own = (lo < 29, lo >= 5)
+
+        def body(i, _):
+            r = pl.ds(pl.multiple_of(i * 8 + 8, 8), 8)
+            for kt in kts:
+                w = pltpu.roll(ty[kt, r, :], 1, 1)
+                tyw[kt, r, :] = w
+                d = dg[kt, r, :] + tx[kt, r, :] + tx[kt, pl.ds(i * 8 + 7, 8), :] + ty[kt, r, :] + w
+                dg[kt, r, :] = d
+                inv = pl.reciprocal(jnp.maximum(d, 0.005), approx=True)
+                inv = inv * (2.0 - jnp.maximum(d, 0.005) * inv)
+                wd = (OMEGA * inv) * (1.0 - ia[kt, r, :])
+                for px in range(2):
+                    if kt < 4 and own[px]:
+                        kd[px, kt, r, :] = wd * sup[px, kt, r, :].astype(F32)
+                    else:
+                        kd[px, kt, r, :] = wd
+            return 0
+
+        lax.fori_loop(lo, hi, body, 0, unroll=unroll)
+
+    lax.fori_loop(1, 33, widen, 0, unroll=2)
+    lax.fori_loop(0, SLABS, dead, 0, unroll=2)
+    diagonal(2, 5, (1, 2), 3)
+    diagonal(5, 29, (1, 2), 4)
+    diagonal(29, 33, (1, 2), 4)
+
+    arrived(coef_sends)
+    for c in goals:
+        c.start()
+    for at in (8, 272):
+        re[at:at + 8, :] = re[at:at + 8, :] + tr[2, at:at + 8, :]
+    widen(0, 0)
+    widen(33, 0)
+    for f, ref in enumerate((tx, ty, dg)):
+        for n in range(SLABS):
+            if n == 0 or n == SLABS - 1:
+                at, away = (0 if n == 0 else 56), 8 * f
+            else:
+                h, i = divmod(n - 1, 16)
+                at, away = 8 + (f * 2 + h) * 8, 8 * i
+            x0, x1 = yd[0, at:at + 8, :], yd[1, at:at + 8, :]
+            r = slice(8 * n + 8, 8 * n + 16)
+            ref[0, r, :] = jnp.where((lane >= 24) & (lane < 32), roll(x0, 24 - away), ref[0, r, :])
+            ref[3, r, :] = jnp.where((lane >= 96) & (lane < 104), roll(x1, 96 - away), ref[3, r, :])
+            x = jnp.where((lane >= 88) & (lane < 96), roll(x0, 88 - away), ref[4, r, :])
+            ref[4, r, :] = jnp.where((lane >= 32) & (lane < 40), roll(x1, 32 - away), x)
+    diagonal(0, 2, (1, 2), 2)
+    diagonal(33, 34, (1, 2), 1)
+    diagonal(0, 5, (0, 3, 4), 5)
+    diagonal(5, 29, (0, 3, 4), 4)
+    diagonal(29, 34, (0, 3, 4), 5)
 
     def keep(first, px):
         def body(i, _):
@@ -352,26 +404,6 @@
             return 0
 
         return body
-
-    lax.fori_loop(0, 29, keep(8, 0), 0, unroll=4)
-    lax.fori_loop(0, 29, keep(48, 1), 0, unroll=4)
-
-    arrived(sends)
-    lax.fori_loop(0, 5, keep(240, 0), 0, unroll=5)
-    lax.fori_loop(0, 5, keep(8, 1), 0, unroll=5)
-
-    def unpack(i, _):
-        r = pl.ds(pl.multiple_of(i * 8 + 8, 8), 8)
-        live = 1.0 - ia[4, r, :]
-        for px in range(2):
-            yr = pl.ds(pl.multiple_of(i * 8 + (272 if px == 0 else 0), 8), 8)
-            from_low, from_high = yl[0, yr, :], yl[1, yr, :]
-            va[px, 4, r, :] = jnp.where(right, from_low, from_high)
-            kept = flip(jnp.where(right, from_high, from_low)) * live
-            kd[px, 4, r, :] = kd[px, 4, r, :] * kept
-        return 0
-
-    lax.fori_loop(0, SLABS, unpack, 0, unroll=17)
 
     def flux_sum(v, px, kt, i):
         r = pl.ds(pl.multiple_of(i * 8 + 8, 8), 8)
@@ -386,7 +418,7 @@
         )
         return mid, total
 
-    def sweep(src, dst):
+    def sweep(src, dst, starts, count, unroll):
         def first(i):
             r = pl.ds(pl.multiple_of(i * 8 + 8, 8), 8)
             raw = []
@@ -408,60 +440,20 @@
                 for px in range(2):
                     dst[px, kt, r, :] = raw[2 * kt + px] * inv
 
+        def firsts(i):
+            return tuple(first(n + i) for n in starts)
+
         def body(i, held):
-            new = first(i)
-            second(i - 1, *held)
+            new = firsts(i)
+            for n, h in zip(starts, held):
+                second(n + i - 1, *h)
             return new
 
-        held = lax.fori_loop(1, SLABS, body, first(0), unroll=3)
-        second(SLABS - 1, *held)
-
-    sweep(va, vb)
-    sweep(vb, va)
-    sweep(va, vb)
+        held = lax.fori_loop(1, count, body, firsts(0), unroll=unroll)
+        for n, h in zip(starts, held):
+            second(n + count - 1, *h)
+
     fin = vb
-
-    def remote2(dx, dy, src, dst, i):
-        return pltpu.make_async_remote_copy(
-            src, dst, s2.at[i], r2.at[i], device_id=(gx + dx, gy + dy), device_id_type=MESH
-        )
-
-    backs = [
-        ((-1, 0), remote2(-1, 0, fin.at[1, pl.ds(0, 4), pl.ds(16, 32), :], out.at[3, :, pl.ds(96, 32), :], 0)),
-        ((1, 0), remote2(1, 0, fin.at[0, pl.ds(0, 4), pl.ds(240, 32), :], out.at[0, :, pl.ds(0, 32), :], 1)),
-    ]
-    for d, c in backs:
-        start(d, [c])
-    for side in range(2):
-        def place_lanes(xs, side=side):
-            m = None
-            for g, x in enumerate(xs):
-                x = roll(x, 32 * g if side == 0 else 32 * g + 32)
-                m = x if m is None else jnp.where(lane < 32 * g, m, x)
-            return m
-
-        rs[side, 0:8, :] = place_lanes([fin[1, 4, 16 + 8 * g:24 + 8 * g, :] for g in range(4)])
-        rs[side, 120:128, :] = place_lanes([fin[0, 4, 240 + 8 * g:248 + 8 * g, :] for g in range(4)])
-
-        def pack_back(i, _, side=side, place_lanes=place_lanes):
-            def at(px, first):
-                return fin[px, 4, pl.ds(pl.multiple_of(first + i * 8, 8), 8), :]
-
-            rs[side, pl.ds(pl.multiple_of(8 + i * 8, 8), 8), :] = place_lanes(
-                [at(0, 16), at(0, 16 + 112), at(1, 48), at(1, 48 + 112)]
-            )
-            return 0
-
-        lax.fori_loop(0, 14, pack_back, 0, unroll=14)
-
-    for dx in (0, 1, -1):
-        for dy, side in ((1, 0), (-1, 1)):
-            at, n = {0: (8, 112), 1: (120, 8), -1: (0, 8)}[dx]
-            i = 2 + {0: 0, 1: 1, -1: 2}[dx] * 2 + side
-            backs.append(
-                ((dx, dy), remote2(dx, dy, rs.at[side, pl.ds(at, n), :], rl.at[side, pl.ds(at, n), :], i))
-            )
-            start((dx, dy), [backs[-1][1]])
 
     def image(h, _):
         for kt in range(5):
@@ -481,7 +473,94 @@
             zz[h, kt] = fold_rows(acc)
         return 0
 
-    lax.fori_loop(0, 8, image, 0)
+
+    def remote2(dx, dy, src, dst, i):
+        return pltpu.make_async_remote_copy(
+            src, dst, s2.at[i], r2.at[i], device_id=(gx + dx, gy + dy), device_id_type=MESH
+        )
+
+    late = ((1, 2, 3, 4, 5, 6, 7, 26, 27, 28), (5, 6, 7, 26, 27, 28, 29, 30, 31, 32))
+    backs = []
+
+    def put(side, at, places):
+        m = None
+        for g, (px, n) in enumerate(places):
+            x = roll(fin[px, 4, 8 * n + 8:8 * n + 16, :], 32 * g if side == 0 else 32 * g + 32)
+            m = x if m is None else jnp.where(lane < 32 * g, m, x)
+        rs[side, at:at + 8, :] = m
+
+    def back(dx, dy, src, dst, i):
+        backs.append(((dx, dy), remote2(dx, dy, src, dst, i)))
+        start((dx, dy), [backs[-1][1]])
+
+    def back_side(dx, at, n, i):
+        for dy, side in ((1, 0), (-1, 1)):
+            back(dx, dy, rs.at[side, pl.ds(at, n), :], rl.at[side, pl.ds(at, n), :], i + side)
+
+    early_places = [[(0, 8 + m), (0, 17 + m), (1, 8 + m), (1, 17 + m)] for m in range(9)]
+    late_places = [[(0, late[0][m]), (0, late[0][m + 5]), (1, late[1][m]), (1, late[1][m + 5])] for m in range(5)]
+
+    arrived(side_sends)
+
+    def apart(m0, m1, n):
+        return jnp.where(
+            lane < 40, roll(m1, -40 * n), jnp.where(lane >= 88, roll(m0, 88 - 40 * n), 0.0)
+        )
+
+    def unpack(i, _):
+        yr = pl.ds(pl.multiple_of(i * 8 + 40, 8), 8)
+        even = pl.ds(pl.multiple_of(i * 8 + 8, 8), 8)
+        odd = pl.ds(pl.multiple_of(i * 8 + 48, 8), 8)
+        m0, m1 = yl[0, yr, :], yl[1, yr, :]
+        va[0, 4, even, :] = apart(m0, m1, 0)
+        va[1, 4, odd, :] = apart(m0, m1, 1)
+        kd[0, 4, even, :] = kd[0, 4, even, :] * apart(m0, m1, 2)
+        return 0
+
+    lax.fori_loop(0, 29, unpack, 0, unroll=8)
+    for i in range(10):
+        m0, m1 = yl[0, 272 + 8 * i:280 + 8 * i, :], yl[1, 272 + 8 * i:280 + 8 * i, :]
+        for n in range(3):
+            at = 48 + 8 * (i + 10 * n)
+            if i + 10 * n < 29:
+                kd[1, 4, at:at + 8, :] = kd[1, 4, at:at + 8, :] * apart(m0, m1, n)
+
+    sweep(va, vb, (6,), 22, 3)
+    sweep(vb, va, (7,), 20, 3)
+    sweep(va, vb, (8,), 18, 3)
+    for side in range(2):
+        for m in range(9):
+            put(side, 8 + 8 * m, early_places[m])
+    back_side(0, 8, 72, 0)
+    lax.fori_loop(2, 6, image, 0)
+
+    arrived(sends)
+    lax.fori_loop(0, 5, keep(240, 0), 0, unroll=5)
+    lax.fori_loop(0, 5, keep(8, 1), 0, unroll=5)
+    for px, at, to in ((1, 0, 8), (0, 352, 240)):
+        for n in range(5):
+            m0, m1 = yl[0, at + 8 * n:at + 8 * n + 8, :], yl[1, at + 8 * n:at + 8 * n + 8, :]
+            r = slice(to + 8 * n, to + 8 * n + 8)
+            va[px, 4, r, :] = jnp.where(right, m0, m1)
+            kd[px, 4, r, :] = kd[px, 4, r, :] * flip(jnp.where(right, m1, m0))
+
+    sweep(va, vb, (0, 28), 6, 2)
+    sweep(vb, va, (0, 27), 7, 2)
+    sweep(va, vb, (0, 26), 8, 2)
+
+    back(-1, 0, fin.at[1, pl.ds(0, 4), pl.ds(16, 32), :], out.at[3, :, pl.ds(96, 32), :], 2)
+    back(1, 0, fin.at[0, pl.ds(0, 4), pl.ds(240, 32), :], out.at[0, :, pl.ds(0, 32), :], 3)
+    for side in range(2):
+        for m in range(5):
+            put(side, 80 + 8 * m, late_places[m])
+        put(side, 0, [(1, n) for n in range(1, 5)])
+        put(side, 120, [(0, n) for n in range(29, 33)])
+    back_side(0, 80, 40, 4)
+    back_side(1, 120, 8, 6)
+    back_side(-1, 0, 8, 8)
+
+    lax.fori_loop(0, 2, image, 0)
+    lax.fori_loop(6, 8, image, 0)
 
     table = jnp.zeros((8, 128), F32)
     bit_x, odd, bit_y = sub // 4, (sub // 2) % 2, sub % 2
@@ -515,8 +594,7 @@
         low = jnp.sum(part[0:4], axis=0, keepdims=True)
         high = jnp.sum(part[4:8], axis=0, keepdims=True)
         table = table + jnp.where(sub == base_x, low, 0.0) + jnp.where(sub == base_x + 1, high, 0.0)
-    tb[1, gx, 0:8, :] = table * (1.0 / 64.0)
-    tb[1, gx, 8:16, :] = target
+    tb[1, gx] = table * (1.0 / 64.0)
 
     hops = []
     for n, (s, t) in enumerate(peers):
@@ -563,22 +641,29 @@
         for g in range(4):
             merge(0, 8 * g, 120, g)
             merge(3, 96 + 8 * g, 0, g)
-        for s in range(28):
-            j, at = (0, 32 + 8 * s) if s < 12 else (2, 8 * (s - 12))
-            merge(j, at, 8 + 8 * (s % 14), s // 14)
-            j, at = (1, 8 * s) if s < 16 else (3, 8 * (s - 16))
-            merge(j, at, 8 + 8 * (s % 14), 2 + s // 14)
+        for first, places in ((8, early_places), (80, late_places)):
+            for m, four in enumerate(places):
+                for g, (px, n) in enumerate(four):
+                    row = 8 * (n - 1)
+                    if px == 0:
+                        j, at = (0, row + 32) if row < 96 else (2, row - 96)
+                    else:
+                        j, at = (1, row - 32) if row < 160 else (3, row - 160)
+                    merge(j, at, first + 8 * m, g)
 
     for t, c in hops:
         @pl.when(exists(0, -t))
         def _(c=c):
             c.wait_recv()
 
+    for c in goals:
+        c.wait_recv()
+
     joined = []
     for s in range(NGX):
-        a = tb[1, s, 0:8, :]
-        below = roll(tb[0, s, 0:8, :], -64)
-        above = roll(tb[2, s, 0:8, :], 64)
+        a = tb[1, s]
+        below = roll(tb[0, s], -64)
+        above = roll(tb[2, s], 64)
         group = lane // 16
         joined.append(a + jnp.where(group == 1, below, 0.0) + jnp.where(group == 4, above, 0.0))
     for s in range(NGX):
@@ -587,7 +672,7 @@
             t = t + jnp.where(sub == 1, sroll(joined[s - 1], -4), 0.0)
         if s < NGX - 1:
             t = t + jnp.where(sub == 4, sroll(joined[s + 1], 4), 0.0)
-        goal = tb[1, s, 8:16, :]
+        goal = tg[s]
         for q in range(4):
             mine = jnp.where(goal == (gx * 4 + q).astype(F32), t, 0.0)
             line = jnp.sum(mine, axis=0, keepdims=True)
@@ -595,7 +680,7 @@
             line = line + pltpu.roll(line, 112, 1)
             rows_out[s * 4 + q:s * 4 + q + 1, :] = line[:, 16:25]
 
-    for (dx, dy), cs in coef_sends + sends:
+    for (dx, dy), cs in coef_sends + side_sends + sends:
         @pl.when(exists(dx, dy))
         def _(cs=cs):
             for c in cs:
@@ -608,6 +693,8 @@
         @pl.when(exists(0, t))
         def _(c=c):
             c.wait_send()
+    for c in goals:
+        c.wait_send()
 
 
 def local(basis, trans, reaction, support, codes, active, owner):
@@ -618,8 +705,8 @@
         kernel,
         name="smooth",
         out_shape=(
-            jax.ShapeDtypeStruct((4, 4, 128, 128), F32),
-            jax.ShapeDtypeStruct((32, 9), F32),
+            pltpu.VMEM((4, 4, 128, 128), F32),
+            pltpu.VMEM((32, 9), F32),
         ),
         in_specs=[anywhere] * 6 + [pl.BlockSpec(memory_space=pltpu.SMEM)],
         out_specs=(vmem, vmem),
@@ -637,7 +724,6 @@
             pltpu.VMEM((5, ROWS, 128), F32),
             pltpu.VMEM((2, 5, ROWS, 128), F32),
             pltpu.VMEM((5, ROWS, 128), F32),
-            pltpu.VMEM((2, 3, 272, 128), F32),
             pltpu.VMEM((2, 4, 40, 128), F32),
             pltpu.VMEM((2, 4, 40, 128), jnp.int32),
             pltpu.VMEM((2, YROWS, 128), F32),
@@ -646,10 +732,11 @@
             pltpu.VMEM((2, CROWS, 128), F32),
             pltpu.VMEM((2, 128, 128), F32),
             pltpu.VMEM((2, 128, 128), F32),
-            pltpu.VMEM((3, NGX, 16, 128), F32),
+            pltpu.VMEM((3, NGX, 8, 128), F32),
+            pltpu.VMEM((NGX, 8, 128), F32),
             pltpu.VMEM((5, ROWS, 128), jnp.int32),
             pltpu.VMEM((8, 5, 8, 128), F32),
-            sem((32,)), sem((24,)), sem((24,)), sem((8,)), sem((8,)), sem((24,)), sem((24,)),
+            sem((32,)), sem((24,)), sem((24,)), sem((10,)), sem((10,)), sem((24,)), sem((24,)), sem((8,)), sem((8,)),
         ],
         compiler_params=pltpu.CompilerParams(
             collective_id=0, has_side_effects=True, vmem_limit_bytes=60 << 20

time: 47.7 us -> 39 us (0.82)
  Pallas kernels: 43.1 us -> 36.5 us
  local copies, waits for them, and re-layouts: 3.69 us -> 1.65 us
    pallas_call x1, Pallas kernels: 43.1 us -> 36.5 us  [local(): pl.pallas_call(kernel, name='smooth', out_shape=(pltpu.VMEM((4, 4, 128, 1...]
    unnamed x2, local copies, waits for them, and re-layouts: 3.69 us -> 1.65 us
where the time goes in v3:
time: 39 us; the launch traced here: 38.8 us
  Pallas kernels  36.5 us (94%)
  local copies, waits for them, and re-layouts  1.65 us (4%)
  between operations  0.64 us (2%)
    pallas_call x1, Pallas kernels, local(): pl.pallas_call(kernel, name='smooth', out_shape=(pltpu.VMEM((4, 4, 128, 1...  36.5 us
    unnamed x2, local copies, waits for them, and re-layouts  1.65 us

profile of v3, /device:TPU:9, one launch (start us, length us, event | category | flops | bytes accessed | tf_op | source)
XLA Modules:
  0.0 38.8 jit_solution(4837912041800845539)
XLA Ops:
  0.6 36.5 %smooth.1 = (f32[4,4,128,128]{3,2,1,0:T(8,128)S(1)}, f32[32,9]{1,0:T(8,128)S(1)}) custom-call(f32[4,4,128,128]{3,2,1,0:T(8,128)} %bitcast.7, f32[3,256,256]{2,1,0:T(8,128)} %bitcast.9, f32[256,256]{1,0:T(8,128)} %bitcast.10, s32[4,4,128,128]{3,2,1,0:T(8,128)} %support.1, s32[4,4,128,128]{3,2,1,0:T(8,128)} %codes.1, s32[4,4,128,128]{3,2,1,0:T(8,128)} %bitcast.8, ...), custom_call_target="tpu_custom_call" | custom-call | tf_op jit(solution)/shard_map/smooth/pallas_call | solution.py:704
  37.1 1.0 %copy.11 = f32[1,4,4,128,128]{4,3,2,1,0:T(8,128)} copy(f32[1,4,4,128,128]{4,3,2,1,0:T(8,128)S(1)} %bitcast.6) | data formatting | bytes 2097152
  38.1 0.7 %copy.9 = f32[32,9]{0,1:T(8,128)} copy(f32[32,9]{1,0:T(8,128)S(1)} %get-tuple-element.7) | data formatting | bytes 2304

commit v4 on v3

--- a/solution.py
+++ b/solution.py
@@ -517,7 +517,7 @@
         kd[0, 4, even, :] = kd[0, 4, even, :] * apart(m0, m1, 2)
         return 0
 
-    lax.fori_loop(0, 29, unpack, 0, unroll=8)
+    lax.fori_loop(0, 29, unpack, 0, unroll=29)
     for i in range(10):
         m0, m1 = yl[0, 272 + 8 * i:280 + 8 * i, :], yl[1, 272 + 8 * i:280 + 8 * i, :]
         for n in range(3):
@@ -559,8 +559,8 @@
     back_side(1, 120, 8, 6)
     back_side(-1, 0, 8, 8)
 
-    lax.fori_loop(0, 2, image, 0)
-    lax.fori_loop(6, 8, image, 0)
+    lax.fori_loop(0, 2, image, 0, unroll=2)
+    lax.fori_loop(6, 8, image, 0, unroll=2)
 
     table = jnp.zeros((8, 128), F32)
     bit_x, odd, bit_y = sub // 4, (sub // 2) % 2, sub % 2

time: 39 us -> 38.6 us (0.990)
  Pallas kernels: 36.5 us -> 35.9 us
    pallas_call x1, Pallas kernels: 36.5 us -> 35.9 us  [local(): pl.pallas_call(kernel, name='smooth', out_shape=(pltpu.VMEM((4, 4, 128, 1...]
where the time goes in v4:
time: 38.6 us; the launch traced here: 38.1 us
  Pallas kernels  35.9 us (93%)
  local copies, waits for them, and re-layouts  1.65 us (4%)
  between operations  0.64 us (2%)
    pallas_call x1, Pallas kernels, local(): pl.pallas_call(kernel, name='smooth', out_shape=(pltpu.VMEM((4, 4, 128, 1...  35.9 us
    unnamed x2, local copies, waits for them, and re-layouts  1.65 us

profile of v4, /device:TPU:9, one launch (start us, length us, event | category | flops | bytes accessed | tf_op | source)
XLA Modules:
  0.0 38.1 jit_solution(9525200482040721705)
XLA Ops:
  0.6 35.9 %smooth.1 = (f32[4,4,128,128]{3,2,1,0:T(8,128)S(1)}, f32[32,9]{1,0:T(8,128)S(1)}) custom-call(f32[4,4,128,128]{3,2,1,0:T(8,128)} %bitcast.7, f32[3,256,256]{2,1,0:T(8,128)} %bitcast.9, f32[256,256]{1,0:T(8,128)} %bitcast.10, s32[4,4,128,128]{3,2,1,0:T(8,128)} %support.1, s32[4,4,128,128]{3,2,1,0:T(8,128)} %codes.1, s32[4,4,128,128]{3,2,1,0:T(8,128)} %bitcast.8, ...), custom_call_target="tpu_custom_call" | custom-call | tf_op jit(solution)/shard_map/smooth/pallas_call | solution.py:704
  36.5 1.0 %copy.11 = f32[1,4,4,128,128]{4,3,2,1,0:T(8,128)} copy(f32[1,4,4,128,128]{4,3,2,1,0:T(8,128)S(1)} %bitcast.6) | data formatting | bytes 2097152
  37.5 0.7 %copy.9 = f32[32,9]{0,1:T(8,128)} copy(f32[32,9]{1,0:T(8,128)S(1)} %get-tuple-element.7) | data formatting | bytes 2304
